TPU v7x, 32 devices: a whole 2x2x4 slice. The times are simulated.
32 devices in a mesh: task: 4 (over y, core), batch: 8 (over z, x).
Axes of the slice: x: 2, y: 2, z: 4, core: 2. Of those that a mesh axis runs over, the one named last changes fastest.
Arguments:
- tokens: bfloat16 [64, 512, 768], P(('task', 'batch')), may hold values from -6 to 6
- out_cot: bfloat16 [64, 512, 768], P(('task', 'batch')), may hold values from -6 to 6
- lengths: int32 [64], P(('task', 'batch')), may hold values from 128 to 512, as said below
- labels: int32 [64], P(('task', 'batch')), may hold values from 0 to 2
- task_ids: int32 [4], P('task'), may hold values from 0 to 7
- task_weights: float32 [4], P('task'), may hold values from 0.5 to 2
- query_weight: bfloat16 [768, 768], replicated, may hold values from -0.21875 to 0.21875
- key_weight: bfloat16 [768, 768], replicated, may hold values from -0.21875 to 0.21875
- value_weight: bfloat16 [768, 768], replicated, may hold values from -0.21875 to 0.21875
- query_bias: bfloat16 [768], replicated, may hold values from -1.5 to 1.5
- value_bias: bfloat16 [768], replicated, may hold values from -1.5 to 1.5
- output_weight: bfloat16 [768, 768], replicated, may hold values from -2.5 to 2.5
- output_bias: bfloat16 [768], replicated, may hold values from -1.5 to 1.5
- norm1_gain: bfloat16 [768], replicated, may hold values from 0.5 to 1.5
- norm1_bias: bfloat16 [768], replicated, may hold values from -1.5 to 1.5
- inner_weight: bfloat16 [768, 3072], replicated, may hold values from -0.21875 to 0.21875
- inner_bias: bfloat16 [3072], replicated, may hold values from -1.5 to 1.5
- outer_weight: bfloat16 [3072, 768], replicated, may hold values from -0.21875 to 0.21875
- outer_bias: bfloat16 [768], replicated, may hold values from -1.5 to 1.5
- norm2_gain: bfloat16 [768], replicated, may hold values from 0.5 to 1.5
- norm2_bias: bfloat16 [768], replicated, may hold values from -1.5 to 1.5
- head_table: bfloat16 [8, 3, 768], replicated, may hold values from -0.625 to 0.625
Outputs:
- block_out: bfloat16 [64, 512, 768], P(('task', 'batch'))
- token_grad: float32 [64, 512, 768], P(('task', 'batch'))
- group_loss: float32 [4], P('task')
- query_weight_grad: float32 [768, 768], P(('task', 'batch'))
- key_weight_grad: float32 [768, 768], P(('task', 'batch'))
- value_weight_grad: float32 [768, 768], P(('task', 'batch'))
- query_bias_grad: float32 [768], P(('task', 'batch'))
- value_bias_grad: float32 [768], P(('task', 'batch'))
- output_weight_grad: float32 [768, 768], P(('task', 'batch'))
- output_bias_grad: float32 [768], P(('task', 'batch'))
- norm1_gain_grad: float32 [768], P(('task', 'batch'))
- norm1_bias_grad: float32 [768], P(('task', 'batch'))
- inner_weight_grad: float32 [768, 3072], P(('task', 'batch'))
- inner_bias_grad: float32 [3072], P(('task', 'batch'))
- outer_weight_grad: float32 [3072, 768], P(('task', 'batch'))
- outer_bias_grad: float32 [768], P(('task', 'batch'))
- norm2_gain_grad: float32 [768], P(('task', 'batch'))
- norm2_bias_grad: float32 [768], P(('task', 'batch'))
- head_table_grad: float32 [8, 3, 768], replicated
Inputs may be any that keep to these rules, and one draw needn't show every extreme that they name: `lengths`: at least one sequence has the full length 512; token 0 of every sequence is inside its length.
All inputs are finite; a program needn't handle non-finite values.
Results may differ from a plain program's by a relative error of at most 0.015.
Values sent between devices are 32-bit elements; how exact they have to be, the bound alone decides.
No kernel may reach another device: no remote copies, remote signals or barrier semaphores. Data moves between devices by JAX's collectives and lax.ppermute only.
A program may use at most 192 MiB of HBM per device.

v0:
```python
import jax
import jax.numpy as jnp
from jax import lax
from jax.sharding import PartitionSpec as P

HD = 64


precise = lax.Precision.HIGHEST
eps_norm = 1e-12


def product(left, right):
    return jnp.dot(left, right, preferred_element_type=jnp.float32)


def product_tn(left, right):
    return lax.dot_general(
        left, right, (((0,), (0,)), ((), ())), preferred_element_type=jnp.float32
    )


def product_nt(left, right):
    return lax.dot_general(
        left, right, (((1,), (1,)), ((), ())), preferred_element_type=jnp.float32
    )


def norm_parts(resid):
    center = resid - jnp.mean(resid, axis=-1, keepdims=True)
    inv_root = lax.rsqrt(jnp.mean(center * center, axis=-1, keepdims=True) + eps_norm)
    return (center * inv_root, inv_root)


def norm_back(grad_out, normed, inv_root, gain):
    scaled = grad_out * gain
    return inv_root * (
        scaled
        - jnp.mean(scaled, axis=-1, keepdims=True)
        - normed * jnp.mean(scaled * normed, axis=-1, keepdims=True)
    )


def gelu_parts(inner):
    cdf_value = 0.5 * (1.0 + lax.erf(inner * 0.7071067811865476))
    pdf_value = jnp.exp(-0.5 * inner * inner) * 0.3989422804014327
    return (inner * cdf_value, cdf_value + inner * pdf_value)


def column_sum(array):
    return jnp.sum(array, axis=0, dtype=jnp.float32)


def per_device(
    tokens,
    out_cot,
    lengths,
    labels,
    task_ids,
    task_weights,
    query_weight,
    key_weight,
    value_weight,
    query_bias,
    value_bias,
    output_weight,
    output_bias,
    norm1_gain,
    norm1_bias,
    inner_weight,
    inner_bias,
    outer_weight,
    outer_bias,
    norm2_gain,
    norm2_bias,
    head_table,
):
    half = jnp.bfloat16
    single = jnp.float32
    seq_count, seq_len, model_width = tokens.shape
    head_count = model_width // HD
    row_count = seq_count * seq_len
    split_shape = (seq_count, seq_len, head_count, HD)
    score_scale = HD ** (-0.5)
    token_rows = tokens.reshape(row_count, model_width)
    query_low = (
        (product(token_rows, query_weight) + query_bias.astype(single))
        .astype(half)
        .reshape(split_shape)
    )
    key_low = product(token_rows, key_weight).astype(half).reshape(split_shape)
    value_low = (
        (product(token_rows, value_weight) + value_bias.astype(single))
        .astype(half)
        .reshape(split_shape)
    )
    key_valid = (jnp.arange(seq_len, dtype=jnp.int32)[None, :] < lengths[:, None])[:, None, None, :]
    scores = (
        jnp.einsum("bqhd,bkhd->bhqk", query_low, key_low, preferred_element_type=single)
        * score_scale
    )
    scores = jnp.where(key_valid, scores, -1e30)
    score_max = jnp.max(scores, axis=-1, keepdims=True)
    exp_scores = jnp.exp(scores - score_max)
    probs_full = exp_scores / jnp.sum(exp_scores, axis=-1, keepdims=True)
    probs_low = probs_full.astype(half)
    ctx_low = (
        jnp.einsum("bhqk,bkhd->bqhd", probs_low, value_low, preferred_element_type=single)
        .astype(half)
        .reshape(row_count, model_width)
    )
    attn = product(ctx_low, output_weight) + output_bias.astype(single)
    gain_one = norm1_gain.astype(single)
    normed1, inv_root1 = norm_parts(token_rows.astype(single) + attn)
    hidden1 = normed1 * gain_one + norm1_bias.astype(single)
    hidden1_low = hidden1.astype(half)
    inner = product(hidden1_low, inner_weight) + inner_bias.astype(single)
    gelu_value, gelu_slope = gelu_parts(inner)
    act_low = gelu_value.astype(half)
    down = product(act_low, outer_weight) + outer_bias.astype(single)
    gain_two = norm2_gain.astype(single)
    normed2, inv_root2 = norm_parts(hidden1 + down)
    final = normed2 * gain_two + norm2_bias.astype(single)
    block_out = final.astype(half).reshape(seq_count, seq_len, model_width)
    task_index = task_ids[0]
    group_weight = task_weights[0]
    chooser = (jnp.arange(head_table.shape[0], dtype=jnp.int32) == task_index).astype(single)
    head_rows = jnp.einsum("t,tcd->cd", chooser, head_table.astype(single), precision=precise)
    cls_low = block_out[:, 0, :]
    logits = product_nt(cls_low, head_rows.astype(half))
    class_count = head_table.shape[1]
    picked_hot = (jnp.arange(class_count, dtype=jnp.int32)[None, :] == labels[:, None]).astype(
        single
    )
    class_lse = jax.nn.logsumexp(logits, axis=-1)
    losses = class_lse - jnp.sum(logits * picked_hot, axis=-1)
    group_seqs = seq_count * lax.axis_size("batch")
    loss_total = lax.psum(jnp.sum(losses), "batch")
    group_loss = (group_weight * loss_total / group_seqs).reshape(1)
    d_logits = (jnp.exp(logits - class_lse[:, None]) - picked_hot) * (group_weight / group_seqs)
    d_head = jnp.dot(d_logits.T, cls_low.astype(single), precision=precise)
    d_cls = jnp.dot(d_logits, head_rows, precision=precise)
    d_final = out_cot.astype(single) * group_weight
    d_final = jnp.concatenate([d_final[:, :1, :] + d_cls[:, None, :], d_final[:, 1:, :]], axis=1)
    d_final = d_final.reshape(row_count, model_width)
    norm2_gain_local = jnp.sum(d_final * normed2, axis=0)
    norm2_bias_local = jnp.sum(d_final, axis=0)
    d_second = norm_back(d_final, normed2, inv_root2, gain_two)
    d_down_low = d_second.astype(half)
    outer_bias_local = column_sum(d_down_low)
    outer_weight_local = product_tn(act_low, d_down_low)
    d_inner_low = (product_nt(d_down_low, outer_weight) * gelu_slope).astype(half)
    inner_bias_local = column_sum(d_inner_low)
    inner_weight_local = product_tn(hidden1_low, d_inner_low)
    d_hidden1 = d_second + product_nt(d_inner_low, inner_weight)
    norm1_gain_local = jnp.sum(d_hidden1 * normed1, axis=0)
    norm1_bias_local = jnp.sum(d_hidden1, axis=0)
    d_first = norm_back(d_hidden1, normed1, inv_root1, gain_one)
    d_attn_low = d_first.astype(half)
    output_bias_local = column_sum(d_attn_low)
    output_weight_local = product_tn(ctx_low, d_attn_low)
    d_ctx_low = product_nt(d_attn_low, output_weight).astype(half).reshape(split_shape)
    d_probs = jnp.einsum("bqhd,bkhd->bhqk", d_ctx_low, value_low, preferred_element_type=single)
    d_value_low = (
        jnp.einsum("bhqk,bqhd->bkhd", probs_low, d_ctx_low, preferred_element_type=single)
        .astype(half)
        .reshape(row_count, model_width)
    )
    d_scores_low = (
        probs_full * (d_probs - jnp.sum(probs_full * d_probs, axis=-1, keepdims=True))
    ).astype(half)
    d_query_low = (
        (
            jnp.einsum("bhqk,bkhd->bqhd", d_scores_low, key_low, preferred_element_type=single)
            * score_scale
        )
        .astype(half)
        .reshape(row_count, model_width)
    )
    d_key_low = (
        (
            jnp.einsum("bhqk,bqhd->bkhd", d_scores_low, query_low, preferred_element_type=single)
            * score_scale
        )
        .astype(half)
        .reshape(row_count, model_width)
    )
    query_weight_local = product_tn(token_rows, d_query_low)
    key_weight_local = product_tn(token_rows, d_key_low)
    value_weight_local = product_tn(token_rows, d_value_low)
    query_bias_local = column_sum(d_query_low)
    value_bias_local = column_sum(d_value_low)
    token_grad = (
        d_first
        + product_nt(d_query_low, query_weight)
        + product_nt(d_key_low, key_weight)
        + product_nt(d_value_low, value_weight)
    ).reshape(seq_count, seq_len, model_width)
    shares = (
        lax.psum_scatter(query_weight_local, ("task", "batch"), scatter_dimension=0, tiled=True),
        lax.psum_scatter(key_weight_local, ("task", "batch"), scatter_dimension=0, tiled=True),
        lax.psum_scatter(value_weight_local, ("task", "batch"), scatter_dimension=0, tiled=True),
        lax.psum_scatter(query_bias_local, ("task", "batch"), scatter_dimension=0, tiled=True),
        lax.psum_scatter(value_bias_local, ("task", "batch"), scatter_dimension=0, tiled=True),
        lax.psum_scatter(output_weight_local, ("task", "batch"), scatter_dimension=0, tiled=True),
        lax.psum_scatter(output_bias_local, ("task", "batch"), scatter_dimension=0, tiled=True),
        lax.psum_scatter(norm1_gain_local, ("task", "batch"), scatter_dimension=0, tiled=True),
        lax.psum_scatter(norm1_bias_local, ("task", "batch"), scatter_dimension=0, tiled=True),
        lax.psum_scatter(inner_weight_local, ("task", "batch"), scatter_dimension=0, tiled=True),
        lax.psum_scatter(inner_bias_local, ("task", "batch"), scatter_dimension=0, tiled=True),
        lax.psum_scatter(outer_weight_local, ("task", "batch"), scatter_dimension=0, tiled=True),
        lax.psum_scatter(outer_bias_local, ("task", "batch"), scatter_dimension=0, tiled=True),
        lax.psum_scatter(norm2_gain_local, ("task", "batch"), scatter_dimension=0, tiled=True),
        lax.psum_scatter(norm2_bias_local, ("task", "batch"), scatter_dimension=0, tiled=True),
    )
    head_local = chooser[:, None, None] * d_head[None, :, :]
    head_table_grad = lax.psum(head_local, ("task", "batch"))
    return (
        block_out,
        token_grad,
        group_loss,
        shares[0],
        shares[1],
        shares[2],
        shares[3],
        shares[4],
        shares[5],
        shares[6],
        shares[7],
        shares[8],
        shares[9],
        shares[10],
        shares[11],
        shares[12],
        shares[13],
        shares[14],
        head_table_grad,
    )


def solution(mesh):
    return jax.shard_map(
        per_device,
        mesh=mesh,
        in_specs=(
            P(("task", "batch"), None, None),
            P(("task", "batch"), None, None),
            P(("task", "batch")),
            P(("task", "batch")),
            P("task"),
            P("task"),
            P(),
            P(),
            P(),
            P(),
            P(),
            P(),
            P(),
            P(),
            P(),
            P(),
            P(),
            P(),
            P(),
            P(),
            P(),
            P(),
        ),
        out_specs=(
            P(("task", "batch"), None, None),
            P(("task", "batch"), None, None),
            P("task"),
            P(("task", "batch"), None),
            P(("task", "batch"), None),
            P(("task", "batch"), None),
            P(("task", "batch")),
            P(("task", "batch")),
            P(("task", "batch"), None),
            P(("task", "batch")),
            P(("task", "batch")),
            P(("task", "batch")),
            P(("task", "batch"), None),
            P(("task", "batch")),
            P(("task", "batch"), None),
            P(("task", "batch")),
            P(("task", "batch")),
            P(("task", "batch")),
            P(),
        ),
        check_vma=False,
    )
```

profile of v0, /device:TPU:0, one launch (start us, length us, event | category | flops | bytes accessed | tf_op | source)
XLA Modules:
  0.0 926.7 jit_solution(16439034421209987240)
XLA Ops:
  15.5 4.3 add_convert_fusion.2
  23.9 4.3 add_convert_fusion.1
  32.3 3.1 convolution_convert_fusion.1
  37.1 2.9 reshape.179
  40.0 15.9 %fusion.74 = (f32[2,12,512]{2,1,0:T(8,128)S(1)}, f32[2,12,512,512]{2,3,1,0:T(8,128)}) fusion(pred[2,512]{1,0:T(4,128)(4,1)S(1)} %iota_compare_fusion, bf16[2,512,12,64]{1,0,3,2:T(2,128)(2,1)S(1)} %reshape.179, bf16[2,512,12,64]{1,0,3,2:T(2,128)(2,1)} %reshape.178), kind=kOutput, calls=%fused_computation.122 | convolution fusion | flops 830472704 | bytes 28361728 | tf_op jit(solution)/shard_map/sub | solution.py:104
  55.9 11.0 %fusion.28 = bf16[2,512,12,64]{1,3,2,0:T(8,128)(2,1)S(1)} fusion(bf16[2,512,12,64]{1,0,3,2:T(2,128)(2,1)} %reshape.177, f32[2,12,512,512]{2,3,1,0:T(8,128)} %get-tuple-element.144, f32[2,12,512]{2,1,0:T(8,128)S(1)} %get-tuple-element.143), kind=kOutput, calls=%fused_computation.64 | convolution fusion | flops 818675712 | bytes 28360704 | tf_op jit(solution)/shard_map/bhqk,bkhd->bqhd/dot_general | solution.py:108
  72.3 9.6 %multiply_convert_fusion.1 = (bf16[1024,3072]{1,0:T(8,128)(2,1)S(1)}, f32[1024,3072]{1,0:T(8,128)}) fusion(f32[3072]{0:T(1024)S(1)} %convert_element_type.138, bf16[768,3072]{1,0:T(8,128)(2,1)S(1)} %bitcast.139, f32[1024,768]{1,0:T(8,128)S(1)} %get-tuple-element.146, f32[768]{0:T(1024)S(1)} %convert_element_type.136, f32[768]{0:T(1024)S(1)} %convert_element_type.135, ...), kind=kOutput, calls=%fused_computation.14 | convolution fusion | flops 4854644736 | bytes 26765312 | tf_op jit(solution)/shard_map/dot_general | solution.py:14
  81.9 5.4 fusion.84
  100.4 12.9 %convert_reduce_fusion = (f32[3072]{0:T(1024)S(1)}, bf16[1024,3072]{1,0:T(8,128)(2,1)S(1)}) fusion(f32[1024,3072]{1,0:T(8,128)} %get-tuple-element.148, f32[3072]{0:T(1024)S(1)} %convert_element_type.138, bf16[3072,768]{1,0:T(8,128)(2,1)S(1)} %bitcast.137, f32[1024,768]{1,0:T(8,128)S(1)} %get-tuple-element.134), kind=kOutput, calls=%fused_computation.13 | convolution fusion | flops 4873516032 | bytes 26763264 | tf_op jit(solution)/shard_map/dot_general | solution.py:24
  113.4 6.1 multiply_reduce_fusion.1
  122.3 2.9 fusion.61
  125.2 4.5 convolution_convert_fusion
  134.0 12.7 %convert_reduce_fusion.3 = (f32[12,64]{1,0:T(8,128)S(1)}, bf16[2,512,12,64]{1,3,2,0:T(8,128)(2,1)S(1)}) fusion(f32[2,12,512,512]{2,3,1,0:T(8,128)} %get-tuple-element.144, f32[2,12,512]{2,1,0:T(8,128)S(1)} %get-tuple-element.143, bf16[2,512,12,64]{1,0,3,2:T(2,128)(2,1)} %reshape.183), kind=kOutput, calls=%fused_computation.32 | convolution fusion | flops 820247808 | bytes 28363776 | tf_op jit(solution)/shard_map/bhqk,bqhd->bkhd/dot_general | solution.py:165
  148.8 2.9 convolution_bitcast_fusion
  151.7 3.1 copy.168
  154.8 18.1 %multiply_reduce_fusion = (f32[2,12,512]{2,1,0:T(8,128)S(1)}, f32[2,12,512,512]{2,3,1,0:T(8,128)}) fusion(f32[2,12,512,512]{2,3,1,0:T(8,128)} %get-tuple-element.144, f32[2,12,512]{2,1,0:T(8,128)S(1)} %get-tuple-element.143, bf16[2,512,12,64]{1,0,3,2:T(2,128)(2,1)} %reshape.177, bf16[2,512,12,64]{1,0,3,2:T(2,128)(2,1)} %reshape.183), kind=kOutput, calls=%fused_computation.2 | convolution fusion | flops 824168448 | bytes 53575680 | tf_op jit(solution)/shard_map/bqhd,bkhd->bhqk/dot_general | solution.py:163
  172.9 17.0 %multiply_convert_fusion = bf16[2,12,512,512]{2,3,1,0:T(8,128)(2,1)S(1)} fusion(f32[2,12,512,512]{2,3,1,0:T(8,128)} %get-tuple-element.155, f32[2,12,512]{2,1,0:T(8,128)S(1)} %get-tuple-element.154, f32[2,12,512,512]{2,3,1,0:T(8,128)} %get-tuple-element.144, f32[2,12,512]{2,1,0:T(8,128)S(1)} %get-tuple-element.143), kind=kLoop, calls=%fused_computation.1 | loop fusion | flops 25165824 | bytes 63012864 | tf_op jit(solution)/shard_map/convert_element_type | solution.py:171
  197.8 2.8 convolution_bitcast_fusion.2
  200.6 3.1 copy.164
  204.0 9.0 fusion.32
  219.0 3.1 copy.166
  222.2 10.4 %fusion.64 = f32[3072,768]{1,0:T(8,128)} fusion(bf16[1024,3072]{1,0:T(8,128)(2,1)} %copy-done.34, f32[1024,768]{1,0:T(8,128)} %copy-done.12), kind=kOutput, calls=%fused_computation.113 | convolution fusion | flops 4832624640 | bytes 18874368 | tf_op jit(solution)/shard_map/dot_general | solution.py:18
  233.3 11.1 %fusion.69 = f32[768,3072]{1,0:T(8,128)} fusion(bf16[1024,3072]{1,0:T(8,128)(2,1)} %copy-done.11, f32[1024,768]{1,0:T(8,128)} %copy-done.5, f32[768]{0:T(1024)S(1)} %copy-done.22, f32[768]{0:T(1024)S(1)} %convert_element_type.135, f32[1024]{0:T(1024)S(1)} %add_rsqrt_fusion.1, f32[1024]{0:T(1024)S(1)} %broadcast_multiply_fusion.5), kind=kOutput, calls=%fused_computation.119 | convolution fusion | flops 4835770368 | bytes 18888704 | tf_op jit(solution)/shard_map/dot_general | solution.py:18
  244.4 23.7 %psum.14 = f32[]{:T(128)} all-reduce(f32[]{:T(128)} %get-tuple-element.137), channel_id=1, replica_groups=mesh['task'=4,'batch'=8] {'batch'}, use_global_device_ids=true, to_apply=%region_15.16 | all-reduce | flops 1 | bytes 8 | tf_op jit(solution)/shard_map/psum | solution.py:138
  268.9 38.2 %all-reduce.9 = (f32[768]{0:T(1024)S(1)}, f32[768]{0:T(1024)S(1)}, f32[768]{0:T(1024)S(1)}, f32[768]{0:T(1024)S(1)}, f32[768]{0:T(1024)S(1)}, /*index=5*/f32[307...) all-reduce(f32[768]{0:T(1024)S(1)} %reduce_sum.224, ...), channel_id=5, replica_groups=mesh['task'=4,'batch'=8] {'task','batch'}, use_global_device_ids=true, to_apply=%region_20.21.clone | all-reduce | flops 9216 | bytes 73728
  312.4 3.4 fusion.86
  318.0 3.2 add_add_fusion
  321.2 104.1 %reduce-scatter.23.cloned.1.call-done = f32[24,768]{1,0:T(8,128)} async-done(((f32[768,768]{1,0:T(8,128)}), f32[24,768]{1,0:T(8,128)}) %reduce-scatter.23.cloned.1.call-update) | async-done | bytes 73744
  425.3 103.8 %reduce-scatter.19.cloned.1.call-done = f32[24,768]{1,0:T(8,128)} async-done(((f32[768,768]{1,0:T(8,128)}), f32[24,768]{1,0:T(8,128)}) %reduce-scatter.19.cloned.1.call-update) | async-done | bytes 73744
  529.1 104.6 %reduce-scatter.21.cloned.1.call-done = f32[24,768]{1,0:T(8,128)} async-done(((f32[768,768]{1,0:T(8,128)}), f32[24,768]{1,0:T(8,128)}) %reduce-scatter.21.cloned.1.call-update) | async-done | bytes 73744
  633.8 140.9 %reduce-scatter.17.cloned.1.call-done = f32[96,768]{1,0:T(8,128)} async-done(((f32[3072,768]{1,0:T(8,128)}), f32[96,768]{1,0:T(8,128)}) %reduce-scatter.17.cloned.1.call-update) | async-done | bytes 294928 | tf_op jit(solution)/shard_map/reduce_scatter | solution.py:211
  774.6 142.1 %reduce-scatter.15.cloned.1.call-done = f32[24,3072]{1,0:T(8,128)} async-done(((f32[768,3072]{1,0:T(8,128)}), f32[24,3072]{1,0:T(8,128)}) %reduce-scatter.15.cloned.1.call-update) | async-done | bytes 294928 | tf_op jit(solution)/shard_map/reduce_scatter | solution.py:209
  (176 shorter events, 68.2 us)
Async XLA Ops:
  7.2 61.7 %copy-start = (bf16[768,768]{1,0:T(8,128)(2,1)S(1)}, bf16[768,768]{1,0:T(8,128)(2,1)}, u32[]{:S(2)}) copy-start(bf16[768,768]{1,0:T(8,128)(2,1)} %param.33) | copy-start | bytes 3538948
  7.2 314.0 %all-reduce.12.cloned.1.call-start = ((), (), s32[]{:S(2)}) async-start(), calls=%async_computation.9 | async-start | bytes 147456 | tf_op jit(solution)/shard_map/psum | solution.py:217
  11.4 70.5 %copy-start.21 = (f32[768]{0:T(1024)}, f32[768]{0:T(1024)S(1)}, u32[]{:S(2)}) copy-start(f32[768]{0:T(1024)S(1)} %convert_element_type.136) | copy-start | bytes 9220
  40.0 15.9 %copy-start.9 = (bf16[2,512,12,64]{1,0,3,2:T(2,128)(2,1)}, bf16[2,512,12,64]{1,0,3,2:T(2,128)(2,1)S(1)}, u32[]{:S(2)}) copy-start(bf16[2,512,12,64]{1,0,3,2:T(2,128)(2,1)S(1)} %reshape.179) | copy-start | bytes 4718596
  68.9 3.3 slice-start.5
  70.7 11.2 %copy-start.5 = (f32[1024,768]{1,0:T(8,128)}, f32[1024,768]{1,0:T(8,128)S(1)}, u32[]{:S(2)}) copy-start(f32[1024,768]{1,0:T(8,128)S(1)} %get-tuple-element.146) | copy-start | bytes 9437188
  70.7 11.2 %slice-start = ((s8[4718592]{0:T(1024)(128)(4,1)}), s8[4194304]{0:T(1024)(128)(4,1)S(1)}, s32[]{:S(2)}) async-start(s8[4718592]{0:T(1024)(128)(4,1)} %bitcast.134), calls=%async_computation.13 | async-start | bytes 8388608
  72.3 9.6 %slice-start.1 = ((s8[4718592]{0:T(1024)(128)(4,1)}), s8[524288]{0:T(1024)(128)(4,1)S(1)}, s32[]{:S(2)}) async-start(s8[4718592]{0:T(1024)(128)(4,1)} %bitcast.134), calls=%async_computation.14 | async-start | bytes 1048576
  81.9 5.5 copy-start.34
  88.0 4.7 copy-start.14
  92.4 228.8 %reduce-scatter.13.cloned.1.call-start = ((), (), s32[]{:S(2)}) async-start(), calls=%async_computation.6 | async-start | bytes 2433024 | tf_op jit(solution)/shard_map/reduce_scatter | solution.py:205
  96.5 3.9 slice-start.2
  98.0 15.4 %slice-start.6 = ((s8[4718592]{0:T(1024)(128)(4,1)}), s8[4194304]{0:T(1024)(128)(4,1)S(1)}, s32[]{:S(2)}) async-start(s8[4718592]{0:T(1024)(128)(4,1)} %bitcast.140), calls=%async_computation.19 | async-start | bytes 8388608
  100.4 13.0 %copy-start.12 = (f32[1024,768]{1,0:T(8,128)}, f32[1024,768]{1,0:T(8,128)S(1)}, u32[]{:S(2)}) copy-start(f32[1024,768]{1,0:T(8,128)S(1)} %get-tuple-element.134) | copy-start | bytes 9437188
  100.4 13.0 %copy-start.6 = (f32[1024,768]{1,0:T(8,128)S(1)}, f32[1024,768]{1,0:T(8,128)}, u32[]{:S(2)}) copy-start(f32[1024,768]{1,0:T(8,128)} %copy-done.5) | copy-start | bytes 9437188
  100.4 13.0 %slice-start.7 = ((s8[4718592]{0:T(1024)(128)(4,1)}), s8[524288]{0:T(1024)(128)(4,1)S(1)}, s32[]{:S(2)}) async-start(s8[4718592]{0:T(1024)(128)(4,1)} %bitcast.140), calls=%async_computation.20 | async-start | bytes 1048576
  113.4 6.1 copy-start.11
  125.2 300.1 %reduce-scatter.23.cloned.1.call-start = ((), (), s32[]{:S(2)}) async-start(), calls=%async_computation.12 | async-start | bytes 2433024
  154.8 374.4 %reduce-scatter.19.cloned.1.call-start = ((), (), s32[]{:S(2)}) async-start(), calls=%async_computation.10 | async-start | bytes 2433024
  172.9 17.0 %copy-start.10 = (bf16[2,512,12,64]{1,0,3,2:T(2,128)(2,1)S(1)}, bf16[2,512,12,64]{1,0,3,2:T(2,128)(2,1)}, u32[]{:S(2)}) copy-start(bf16[2,512,12,64]{1,0,3,2:T(2,128)(2,1)} %copy-done.9) | copy-start | bytes 4718596
  190.0 4.6 copy-start.2
  203.7 430.1 %reduce-scatter.21.cloned.1.call-start = ((), (), s32[]{:S(2)}) async-start(), calls=%async_computation.11 | async-start | bytes 2433024
  212.9 3.3 copy-start.32
  222.2 552.5 %reduce-scatter.17.cloned.1.call-start = ((), (), s32[]{:S(2)}) async-start(), calls=%async_computation.8 | async-start | bytes 9732096 | tf_op jit(solution)/shard_map/reduce_scatter | solution.py:211
  232.6 684.1 %reduce-scatter.15.cloned.1.call-start = ((), (), s32[]{:S(2)}) async-start(), calls=%async_computation.7 | async-start | bytes 9732096 | tf_op jit(solution)/shard_map/reduce_scatter | solution.py:209
  244.4 24.5 %copy-start.25 = (f32[768]{0:T(1024)S(1)}, f32[768]{0:T(1024)}, u32[]{:S(2)}) copy-start(f32[768]{0:T(1024)} %get-tuple-element.131) | copy-start | bytes 9220
  244.4 24.5 %copy-start.26 = (f32[768]{0:T(1024)S(1)}, f32[768]{0:T(1024)}, u32[]{:S(2)}) copy-start(f32[768]{0:T(1024)} %get-tuple-element.141) | copy-start | bytes 9220
  244.4 24.5 %copy-start.24 = (f32[768]{0:T(1024)S(1)}, f32[768]{0:T(1024)}, u32[]{:S(2)}) copy-start(f32[768]{0:T(1024)} %get-tuple-element.133) | copy-start | bytes 9220
  244.4 24.5 %copy-start.27 = (f32[768]{0:T(1024)S(1)}, f32[768]{0:T(1024)}, u32[]{:S(2)}) copy-start(f32[768]{0:T(1024)} %get-tuple-element.114) | copy-start | bytes 9220
  312.4 3.4 copy-start.19
  312.4 3.4 copy-start.33
  318.0 600.3 %copy-start.1 = (bf16[768,768]{1,0:T(8,128)(2,1)S(1)}, bf16[768,768]{1,0:T(8,128)(2,1)}, u32[]{:S(2)}) copy-start(bf16[768,768]{1,0:T(8,128)(2,1)} %param.33) | copy-start | bytes 3538948
  (18 other events, 35.5 us)
Sparse Core Ops, SparseCore 0:
  92.5 121.0 all-reduce.11
  219.5 101.0 reduce-scatter.12
  327.3 97.9 reduce-scatter.22
  431.0 98.0 reduce-scatter.18
  535.7 98.0 reduce-scatter.20
  640.1 134.4 reduce-scatter.16
  782.1 134.5 reduce-scatter.14
where the time goes:
time: 935 us; the launch traced here: 927 us
  waiting for transfers between devices  596 us (64%)
  matrix products  163 us (17%)
  blocking collectives  61.9 us (7%)
  local copies, waits for them, and re-layouts  53.1 us (6%)
  other arithmetic  34.5 us (4%)
  between operations  18.5 us (2%)
    unnamed x10, waiting for transfers between devices  313 us
    reduce_scatter x1, waiting for transfers between devices, per_device(): lax.psum_scatter(inner_weight_local, ('task', 'batch'), scatter_dimension...  142 us
    reduce_scatter x1, waiting for transfers between devices, per_device(): lax.psum_scatter(outer_weight_local, ('task', 'batch'), scatter_dimension...  141 us
    unnamed x1, blocking collectives  38.2 us
    dot_general x6, matrix products, product_tn(): lax.dot_general(left, right, (((0,), (0,)), ((), ())), preferred_element_...  32.9 us
    dot_general x7, matrix products, product_nt(): lax.dot_general(left, right, (((1,), (1,)), ((), ())), preferred_element_...  31.7 us
    unnamed x104, local copies, waits for them, and re-layouts  29.5 us
    dot_general x6, matrix products, product(): return jnp.dot(left, right, preferred_element_type=jnp.float32)  28.4 us
  transfers between devices with their start and end apart: 7, of which 5 were waited for; matrix products, arithmetic and copies ran while one was open for 17% of the time, Pallas kernels for 0%

commit v1 on v0

v1 whole, which is shorter than its diff:
```python
import functools

import jax
import jax.numpy as jnp
from jax import lax
from jax.experimental import pallas as pl
from jax.experimental.pallas import tpu as pltpu
from jax.sharding import PartitionSpec as P

HD = 64
TILE = 256
ALL_AXES = ("task", "batch")
NN = (((1,), (0,)), ((), ()))
NT = (((1,), (1,)), ((), ()))
TN = (((0,), (0,)), ((), ()))
half = jnp.bfloat16
single = jnp.float32
eps_norm = 1e-12


def dot(left, right, dims=NN):
    return lax.dot_general(left, right, dims, preferred_element_type=single)


def params(megabytes=56):
    return pltpu.CompilerParams(vmem_limit_bytes=megabytes << 20)


def cost(flops):
    return pl.CostEstimate(flops=int(flops), bytes_accessed=1 << 20, transcendentals=0)


def spec(shape, index):
    return pl.BlockSpec(shape, index)


ANY = pl.BlockSpec(memory_space=pl.ANY)
SMEM = pl.BlockSpec(memory_space=pltpu.SMEM)
TOKEN = jax.ShapeDtypeStruct((8, 128), single)


def pair_operands(q, k, h, n, scale):
    rows = q.shape[0]
    lane = lax.broadcasted_iota(jnp.int32, (rows, 128), 1)
    row = lax.broadcasted_iota(jnp.int32, (rows, 128), 0)
    pair, parity = h // 2, h % 2
    inside = (lane // HD) == parity
    spare = HD * (1 - parity)
    q_pair = q[:, pair * 128 : pair * 128 + 128].astype(single) * scale
    k_pair = k[:, pair * 128 : pair * 128 + 128].astype(single)
    q_one = jnp.where(inside, q_pair, jnp.where(lane == spare, 1.0, 0.0)).astype(half)
    k_one = jnp.where(inside, k_pair, jnp.where((lane == spare) & (row >= n), -1e30, 0.0)).astype(half)
    return q_one, k_one


def attention_kernel(
    n_ref, x_ref, wq_ref, wk_ref, wv_ref, bq_ref, bv_ref, q_ref, k_ref, v_ref, ctx_ref, ctxt_ref, lse_ref
):
    n = n_ref[pl.program_id(0)]
    x = x_ref[0]
    heads = wq_ref.shape[1] // HD
    q = (dot(x, wq_ref[...]) + bq_ref[...].astype(single)).astype(half)
    k = dot(x, wk_ref[...]).astype(half)
    v = (dot(x, wv_ref[...]) + bv_ref[...].astype(single)).astype(half)
    q_ref[0] = q
    k_ref[0] = k
    v_ref[0] = v
    vt = v.T
    scores = []
    for h in range(heads):
        q_one, k_one = pair_operands(q, k, h, n, HD**-0.5)
        scores.append(dot(k_one, q_one, NT))
    weights = []
    for s in scores:
        top = jnp.max(s, axis=0, keepdims=True)
        e = jnp.exp(s - top)
        weights.append((e.astype(half), top, jnp.sum(e, axis=0, keepdims=True)))
    for h, (e, top, total) in enumerate(weights):
        c = dot(vt[h * HD : (h + 1) * HD], e) * (1.0 / total)
        ctxt_ref[h * HD : (h + 1) * HD, :] = c.astype(half)
        lse_ref[0, 0, h : h + 1, :] = top + jnp.log(total)
    ctx_ref[0] = ctxt_ref[...].T


def attention(tokens, lengths, wq, wk, wv, bq, bv):
    seqs, length, width = tokens.shape
    quads = width // 256
    rows = spec((1, length, 256), lambda s, g, n: (s, 0, g))
    w = spec((width, 256), lambda s, g, n: (0, g))
    b = spec((1, 256), lambda s, g, n: (0, g))
    return pl.pallas_call(
        attention_kernel,
        grid_spec=pltpu.PrefetchScalarGridSpec(
            num_scalar_prefetch=1,
            grid=(seqs, quads),
            in_specs=[spec((1, length, width), lambda s, g, n: (s, 0, 0)), w, w, w, b, b],
            out_specs=[
                rows,
                rows,
                rows,
                rows,
                spec((256, length), lambda s, g, n: (g, s)),
                spec((1, 1, 8, length), lambda s, g, n: (s, g, 0, 0)),
            ],
        ),
        out_shape=[jax.ShapeDtypeStruct(tokens.shape, half)] * 4
        + [
            jax.ShapeDtypeStruct((width, seqs * length), half),
            jax.ShapeDtypeStruct((seqs, quads, 8, length), single),
        ],
        compiler_params=params(40),
        cost_estimate=cost(15e9),
        name="attention_forward",
    )(lengths, tokens, wq, wk, wv, bq.reshape(1, -1), bv.reshape(1, -1))


def norm_parts(resid):
    center = resid - jnp.mean(resid, axis=-1, keepdims=True)
    inv_root = lax.rsqrt(jnp.mean(center * center, axis=-1, keepdims=True) + eps_norm)
    return center * inv_root, inv_root


def norm_back(grad_out, normed, inv_root, gain):
    scaled = grad_out * gain
    return inv_root * (
        scaled
        - jnp.mean(scaled, axis=-1, keepdims=True)
        - normed * jnp.mean(scaled * normed, axis=-1, keepdims=True)
    )


def gelu_parts(u):
    cdf = 0.5 * (1.0 + lax.erf(u * 0.7071067811865476))
    pdf = jnp.exp(-0.5 * u * u) * 0.3989422804014327
    return u * cdf, cdf + u * pdf


def column_sum(array):
    return jnp.sum(array, axis=0, keepdims=True)


def middle_kernel(
    task_ref,
    label_ref,
    weight_ref,
    x_ref,
    ctx_ref,
    cot_ref,
    wo_ref,
    wi_ref,
    wd_ref,
    vec_ref,
    bi_ref,
    head_ref,
    out_ref,
    normed1_ref,
    root1_ref,
    h1t_ref,
    act_ref,
    slope_ref,
    dr2_ref,
    ddown_ref,
    sums_ref,
    *,
    tiles_per_seq,
    group_seqs,
):
    step = pl.program_id(0)
    vec = vec_ref[...]
    bo, g1, b1, bd, g2, b2 = [vec[i : i + 1] for i in range(6)]
    x = x_ref[...].astype(single)
    normed1, root1 = norm_parts(x + dot(ctx_ref[...], wo_ref[...]) + bo)
    normed1_ref[...] = normed1
    root1_ref[...] = jnp.broadcast_to(root1, root1_ref.shape)
    hidden1 = normed1 * g1 + b1
    h1 = hidden1.astype(half)
    h1t_ref[...] = h1.T
    ff = wi_ref.shape[1]
    part = 768
    down = None
    for j in range(0, ff, part):
        inner = dot(h1, wi_ref[:, j : j + part]) + bi_ref[:, j : j + part].astype(single)
        value, slope = gelu_parts(inner)
        act = value.astype(half)
        act_ref[:, j : j + part] = act
        slope_ref[:, j : j + part] = slope.astype(half)
        term = dot(act, wd_ref[j : j + part, :])
        down = term if down is None else down + term
    normed2, root2 = norm_parts(hidden1 + down + bd)
    final = normed2 * g2 + b2
    low = final.astype(half)
    out_ref[...] = low
    w = weight_ref[0]
    cls = low[0:1].astype(single)
    head = head_ref[0].astype(single)
    classes = head.shape[0]
    logits = [jnp.sum(cls * head[c : c + 1], axis=1, keepdims=True) for c in range(classes)]
    top = functools.reduce(jnp.maximum, logits)
    lse = top + jnp.log(sum(jnp.exp(v - top) for v in logits))
    label = label_ref[step // tiles_per_seq]
    first = jnp.where(step % tiles_per_seq == 0, 1.0, 0.0)
    picked = sum(jnp.where(label == c, v, 0.0) for c, v in enumerate(logits))
    slopes = [
        (jnp.exp(v - lse) - jnp.where(label == c, 1.0, 0.0)) * (w / group_seqs * first)
        for c, v in enumerate(logits)
    ]
    d_cls = sum(s * head[c : c + 1] for c, s in enumerate(slopes))
    row = lax.broadcasted_iota(jnp.int32, final.shape, 0)
    d_final = cot_ref[...].astype(single) * w + jnp.where(row == 0, d_cls, 0.0)
    dr2 = norm_back(d_final, normed2, root2, g2)
    dr2_ref[...] = dr2
    ddown = dr2.astype(half)
    ddown_ref[...] = ddown

    @pl.when(step == 0)
    def _():
        sums_ref[...] = jnp.zeros_like(sums_ref)

    sums_ref[0:1] += column_sum(d_final * normed2)
    sums_ref[1:2] += column_sum(d_final)
    sums_ref[2:3] += column_sum(ddown.astype(single))
    for c in range(classes):
        sums_ref[3 + c : 4 + c] += slopes[c] * cls
    sums_ref[7:8] += jnp.broadcast_to((lse - picked) * (w / group_seqs * first), cls.shape)


def middle(tokens, ctx, cot, labels, task_ids, task_weights, wo, wi, wd, vec, bi, head_table, group_seqs):
    seqs, length, width = tokens.shape
    rows = seqs * length
    ff = wi.shape[1]
    classes = head_table.shape[1]
    assert classes <= 4
    tile = spec((TILE, width), lambda i, t, l: (i, 0))
    wide = spec((TILE, ff), lambda i, t, l: (i, 0))

    def whole(shape):
        return spec(shape, lambda i, t, l: (0, 0))

    return pl.pallas_call(
        functools.partial(middle_kernel, tiles_per_seq=length // TILE, group_seqs=group_seqs),
        grid_spec=pltpu.PrefetchScalarGridSpec(
            num_scalar_prefetch=2,
            grid=(rows // TILE,),
            in_specs=[
                SMEM,
                tile,
                tile,
                tile,
                whole((width, width)),
                whole((width, ff)),
                whole((ff, width)),
                whole((8, width)),
                whole((1, ff)),
                spec((1, classes, width), lambda i, t, l: (t[0], 0, 0)),
            ],
            out_specs=[
                tile,
                tile,
                spec((TILE, 128), lambda i, t, l: (i, 0)),
                spec((width, TILE), lambda i, t, l: (0, i)),
                wide,
                wide,
                tile,
                tile,
                whole((8, width)),
            ],
        ),
        out_shape=[
            jax.ShapeDtypeStruct((rows, width), half),
            jax.ShapeDtypeStruct((rows, width), single),
            jax.ShapeDtypeStruct((rows, 128), single),
            jax.ShapeDtypeStruct((width, rows), half),
            jax.ShapeDtypeStruct((rows, ff), half),
            jax.ShapeDtypeStruct((rows, ff), half),
            jax.ShapeDtypeStruct((rows, width), single),
            jax.ShapeDtypeStruct((rows, width), half),
            jax.ShapeDtypeStruct((8, width), single),
        ],
        compiler_params=params(),
        cost_estimate=cost(20e9),
        name="middle_forward",
    )(
        task_ids,
        labels,
        task_weights,
        tokens.reshape(rows, width),
        ctx.reshape(rows, width),
        cot.reshape(rows, width),
        wo,
        wi,
        wd,
        vec,
        bi.reshape(1, -1),
        head_table,
    )


def inner_grad_kernel(token_ref, ddown_ref, wd_ref, slope_ref, dinner_ref, bias_ref):
    d = dot(ddown_ref[...], wd_ref[...], NT) * slope_ref[...].astype(single)
    low = d.astype(half)
    dinner_ref[...] = low
    bias_ref[...] = column_sum(low.astype(single))


def inner_grad(token, ddown, wd, slope):
    rows, width = ddown.shape
    ff = wd.shape[0]
    part = 768
    return pl.pallas_call(
        inner_grad_kernel,
        grid=(ff // part,),
        in_specs=[
            ANY,
            spec((rows, width), lambda j: (0, 0)),
            spec((part, width), lambda j: (j, 0)),
            spec((rows, part), lambda j: (0, j)),
        ],
        out_specs=[spec((rows, part), lambda j: (0, j)), spec((1, part), lambda j: (0, j))],
        out_shape=[jax.ShapeDtypeStruct((rows, ff), half), jax.ShapeDtypeStruct((1, ff), single)],
        compiler_params=params(),
        cost_estimate=cost(20e9),
        name="inner_grad",
    )(token, ddown, wd, slope)


def first_norm_kernel(
    pos_ref,
    token_ref,
    dinner_ref,
    wi_ref,
    dr2_ref,
    normed1_ref,
    root1_ref,
    wo_ref,
    ctxt_ref,
    vec_ref,
    x_ref,
    dr1_ref,
    dctx_ref,
    xt_ref,
    send_ref,
    keep_ref,
    sums_ref,
):
    step = pl.program_id(0)
    g1 = vec_ref[1:2]
    normed1 = normed1_ref[...]
    dh1 = dr2_ref[...] + dot(dinner_ref[...], wi_ref[...], NT)
    dr1 = norm_back(dh1, normed1, root1_ref[:, 0:1], g1)
    dr1_ref[...] = dr1
    dattn = dr1.astype(half)
    dctx_ref[...] = dot(dattn, wo_ref[...], NT).astype(half)
    xt_ref[...] = x_ref[...].T

    @pl.when(step == 0)
    def _():
        sums_ref[...] = jnp.zeros_like(sums_ref)
        send_ref[...] = jnp.zeros_like(send_ref)
        keep_ref[...] = jnp.zeros_like(keep_ref)

    sums_ref[0:1] += column_sum(dh1 * normed1)
    sums_ref[1:2] += column_sum(dh1)
    sums_ref[2:3] += column_sum(dattn.astype(single))
    me = pos_ref[1]
    part = dot(ctxt_ref[...], dattn)
    quarter = part.shape[0] // 4
    for y in range(2):
        zero = part[2 * y * quarter : (2 * y + 1) * quarter]
        one = part[(2 * y + 1) * quarter : (2 * y + 2) * quarter]
        send_ref[y * quarter : (y + 1) * quarter] += jnp.where(me == 0, one, zero)
        keep_ref[y * quarter : (y + 1) * quarter] += jnp.where(me == 0, zero, one)


def first_norm(pos, token, dinner, wi, dr2, normed1, root1, wo, ctxt, vec, x):
    rows, width = dr2.shape
    ff = wi.shape[1]
    tile = spec((TILE, width), lambda i, p: (i, 0))

    def whole(shape):
        return spec(shape, lambda i, p: (0, 0))

    return pl.pallas_call(
        first_norm_kernel,
        grid_spec=pltpu.PrefetchScalarGridSpec(
            num_scalar_prefetch=1,
            grid=(rows // TILE,),
            in_specs=[
                ANY,
                spec((TILE, ff), lambda i, p: (i, 0)),
                whole((width, ff)),
                tile,
                tile,
                spec((TILE, 128), lambda i, p: (i, 0)),
                whole((width, width)),
                spec((width, TILE), lambda i, p: (0, i)),
                whole((8, width)),
                tile,
            ],
            out_specs=[
                tile,
                tile,
                spec((width, TILE), lambda i, p: (0, i)),
                whole((width // 2, width)),
                whole((width // 2, width)),
                whole((8, width)),
            ],
        ),
        out_shape=[
            jax.ShapeDtypeStruct((rows, width), single),
            jax.ShapeDtypeStruct((rows, width), half),
            jax.ShapeDtypeStruct((width, rows), half),
            jax.ShapeDtypeStruct((width // 2, width), single),
            jax.ShapeDtypeStruct((width // 2, width), single),
            jax.ShapeDtypeStruct((8, width), single),
        ],
        compiler_params=params(),
        cost_estimate=cost(20e9),
        name="first_norm_back",
    )(pos, token, dinner, wi, dr2, normed1, root1, wo, ctxt, vec, x)


def attention_back_kernel(
    n_ref, token_ref, q_ref, k_ref, v_ref, ctx_ref, dctx_ref, lse_ref, dq_ref, dk_ref, dv_ref, sums_ref, dqt_ref
):
    n = n_ref[pl.program_id(0)]
    q, k, v, dctx = q_ref[0], k_ref[0], v_ref[0], dctx_ref[0]
    rows, width = q.shape
    heads = width // HD
    lane = lax.broadcasted_iota(jnp.int32, (rows, 128), 1)
    kt = k.T
    prod_t = (ctx_ref[0].astype(single) * dctx.astype(single)).T
    scale = HD**-0.5
    for pair in range(heads // 2):
        cols = slice(pair * 128, pair * 128 + 128)
        q_pair, v_pair, d_pair = q[:, cols], v[:, cols], dctx[:, cols]
        dks, dvs = [], []
        for parity in range(2):
            h = pair * 2 + parity
            q_one, k_one = pair_operands(q, k, h, n, scale)
            p = jnp.exp(dot(k_one, q_one, NT) - lse_ref[0, 0, h : h + 1, :])
            inside = (lane // HD) == parity
            v_one = jnp.where(inside, v_pair.astype(single), 0.0).astype(half)
            dp = dot(v_one, d_pair, NT)
            delta = jnp.sum(prod_t[h * HD : (h + 1) * HD], axis=0, keepdims=True)
            ds = (p * (dp - delta)).astype(half)
            dvs.append(dot(p.astype(half), d_pair))
            dks.append(dot(ds, q_pair))
            dqt_ref[h * HD : (h + 1) * HD, :] = (dot(kt[h * HD : (h + 1) * HD], ds) * scale).astype(half)
        low_half = lane < HD
        dk_ref[0, :, cols] = (jnp.where(low_half, dks[0], dks[1]) * scale).astype(half)
        dv_ref[0, :, cols] = jnp.where(low_half, dvs[0], dvs[1]).astype(half)
    dq = dqt_ref[...].T
    dq_ref[0] = dq
    sums_ref[0, 0, 0:1, :] = column_sum(dq.astype(single))
    sums_ref[0, 0, 1:2, :] = column_sum(dv_ref[0].astype(single))


def attention_back(lengths, token, q, k, v, ctx, dctx, lse):
    seqs, length, width = q.shape
    quads = width // 256
    rows = spec((1, length, 256), lambda s, g, n: (s, 0, g))
    return pl.pallas_call(
        attention_back_kernel,
        grid_spec=pltpu.PrefetchScalarGridSpec(
            num_scalar_prefetch=1,
            grid=(seqs, quads),
            in_specs=[ANY, rows, rows, rows, rows, rows, spec((1, 1, 8, length), lambda s, g, n: (s, g, 0, 0))],
            out_specs=[rows, rows, rows, spec((1, 1, 8, 256), lambda s, g, n: (s, g, 0, 0))],
            scratch_shapes=[pltpu.VMEM((256, length), half)],
        ),
        out_shape=[jax.ShapeDtypeStruct(q.shape, half)] * 3 + [jax.ShapeDtypeStruct((seqs, quads, 8, 256), single)],
        compiler_params=params(),
        cost_estimate=cost(20e9),
        name="attention_back",
    )(lengths, token, q, k, v, ctx, dctx.reshape(q.shape), lse)


def outer_send_kernel(pos_ref, act_ref, ddown_ref, send_ref):
    send_ref[0] = dot(act_ref[...], ddown_ref[...], TN)


def outer_send(pos, act, ddown, other):
    rows, width = ddown.shape
    ff = act.shape[1]
    part = ff // 4
    return pl.pallas_call(
        outer_send_kernel,
        grid_spec=pltpu.PrefetchScalarGridSpec(
            num_scalar_prefetch=1,
            grid=(2,),
            in_specs=[
                spec((rows, part), lambda y, p: (0, 2 * y + (1 - p[1] if other else p[1]))),
                spec((rows, width), lambda y, p: (0, 0)),
            ],
            out_specs=spec((1, part, width), lambda y, p: (y, 0, 0)),
        ),
        out_shape=jax.ShapeDtypeStruct((2, part, width), single),
        compiler_params=params(),
        cost_estimate=cost(10e9),
        name="outer_weight_send",
    )(pos, act, ddown)


def split_x(pos, block, rows, cols, at, sx, kx, to):
    me = pos[2]
    for z in range(4):
        zero = block[(2 * z) * rows : (2 * z + 1) * rows, cols]
        one = block[(2 * z + 1) * rows : (2 * z + 2) * rows, cols]
        sx[at + (z, slice(None), to)] = jnp.where(me == 0, one, zero)
        kx[at + (z, slice(None), to)] = jnp.where(me == 0, zero, one)


def split_z(pos, block, rows, cols, at, sz, kz, to):
    side = pos[3]
    for x in range(2):
        zs = [block[(2 * z + x) * rows : (2 * z + x + 1) * rows, cols] for z in range(4)]
        for hi, (even, odd) in enumerate(((0, 1), (3, 2))):
            sz[at + (hi, x, slice(None), to)] = jnp.where(side == 0, zs[odd], zs[even])
            kz[at + (hi, x, slice(None), to)] = jnp.where(side == 0, zs[even], zs[odd])


def outer_keep_kernel(pos_ref, token_ref, act_ref, ddown_ref, got_ref, sx_ref, kx_ref, sy_ref, ky_ref, sz_ref, kz_ref, tok_ref):
    y = pl.program_id(0)
    block = dot(act_ref[...], ddown_ref[...], TN) + got_ref[0]
    rows = block.shape[0] // 8
    third = block.shape[1] // 3
    split_x(pos_ref, block, rows, slice(0, third), (0,), sx_ref, kx_ref, slice(None))
    mid = block[:, third : 2 * third].reshape(4, 2, rows, third)

    @pl.when(y == pos_ref[0])
    def _():
        ky_ref[...] = mid

    @pl.when(y != pos_ref[0])
    def _():
        sy_ref[...] = mid

    split_z(pos_ref, block, rows, slice(2 * third, 3 * third), (0,), sz_ref, kz_ref, slice(None))
    tok_ref[...] = block[0:8, 0:128]


def outer_keep(pos, token, act, ddown, got):
    rows, width = ddown.shape
    ff = act.shape[1]
    part = ff // 4
    r, third = part // 8, width // 3
    xs = spec((1, 4, r, third), lambda y, p: (y, 0, 0, 0))
    ys = spec((4, 2, r, third), lambda y, p: (0, 0, 0, 0))
    zs = spec((1, 2, 2, r, third), lambda y, p: (y, 0, 0, 0, 0))
    return pl.pallas_call(
        outer_keep_kernel,
        grid_spec=pltpu.PrefetchScalarGridSpec(
            num_scalar_prefetch=1,
            grid=(2,),
            in_specs=[
                ANY,
                spec((rows, part), lambda y, p: (0, 2 * y + p[1])),
                spec((rows, width), lambda y, p: (0, 0)),
                spec((1, part, width), lambda y, p: (y, 0, 0)),
            ],
            out_specs=[xs, xs, ys, ys, zs, zs, spec((8, 128), lambda y, p: (0, 0))],
        ),
        out_shape=[jax.ShapeDtypeStruct((2, 4, r, third), single)] * 2
        + [jax.ShapeDtypeStruct((4, 2, r, third), single)] * 2
        + [jax.ShapeDtypeStruct((2, 2, 2, r, third), single)] * 2
        + [TOKEN],
        compiler_params=params(),
        cost_estimate=cost(10e9),
        name="outer_weight_keep",
    )(pos, token, act, ddown, got)


def row_half(left_ref, me):
    return jnp.concatenate([left_ref[0, me], left_ref[1, me]], axis=0)


def rows_send_kernel(pos_ref, token_ref, left_ref, right_ref, send_ref, tok_ref, *, other):
    me = 1 - pos_ref[1] if other else pos_ref[1]
    send_ref[0] = dot(row_half(left_ref, me), right_ref[...])
    tok_ref[...] = send_ref[0, 0:8, 0:128]


def rows_send(pos, token, left_t, right, other, parts):
    width, rows = left_t.shape
    columns = right.shape[1] // parts
    return pl.pallas_call(
        functools.partial(rows_send_kernel, other=other),
        grid_spec=pltpu.PrefetchScalarGridSpec(
            num_scalar_prefetch=1,
            grid=(parts,),
            in_specs=[
                ANY,
                spec((2, 2, width // 4, rows), lambda j, p: (0, 0, 0, 0)),
                spec((rows, columns), lambda j, p: (0, j)),
            ],
            out_specs=[
                spec((1, width // 2, columns), lambda j, p: (j, 0, 0)),
                spec((8, 128), lambda j, p: (0, 0)),
            ],
        ),
        out_shape=[jax.ShapeDtypeStruct((parts, width // 2, columns), single), TOKEN],
        compiler_params=params(),
        cost_estimate=cost(10e9),
        name="weight_rows_send",
    )(pos, token, left_t.reshape(2, 2, width // 4, rows), right)


def inner_keep_kernel(
    pos_ref,
    token_ref,
    left_ref,
    right_ref,
    got_ref,
    okeep_ref,
    ogot_ref,
    sx_ref,
    kx_ref,
    sy_ref,
    ky_ref,
    sz_ref,
    kz_ref,
    tok_ref,
):
    step = pl.program_id(0)
    block = dot(row_half(left_ref, pos_ref[1]), right_ref[...]) + got_ref[0]
    count, columns = block.shape
    rows = count // 16
    tok_ref[...] = block[0:8, 0:128]
    out_half = okeep_ref.shape[1] // 2

    @pl.when(step == 0)
    def _():
        extra = okeep_ref[:, :out_half] + ogot_ref[:, :out_half]
        for y in range(2):
            sub = slice(y * 8 * rows, (y + 1) * 8 * rows)
            split_x(pos_ref, block[sub], rows, slice(None), (y,), sx_ref, kx_ref, slice(0, columns))
            split_x(pos_ref, extra[sub], rows, slice(None), (y,), sx_ref, kx_ref, slice(columns, columns + out_half))

    @pl.when(step == 1)
    def _():
        extra = okeep_ref[:, out_half:] + ogot_ref[:, out_half:]
        me = pos_ref[0]
        for data, to in ((block, slice(0, columns)), (extra, slice(columns, columns + out_half))):
            zero = data[: 8 * rows].reshape(4, 2, rows, data.shape[1])
            one = data[8 * rows :].reshape(4, 2, rows, data.shape[1])
            sy_ref[:, :, :, to] = jnp.where(me == 0, one, zero)
            ky_ref[:, :, :, to] = jnp.where(me == 0, zero, one)

    @pl.when(step == 2)
    def _():
        for y in range(2):
            sub = slice(y * 8 * rows, (y + 1) * 8 * rows)
            split_z(pos_ref, block[sub], rows, slice(None), (y,), sz_ref, kz_ref, slice(None))


def inner_keep(pos, token, left_t, right, got, out_keep, out_got):
    width, rows = left_t.shape
    columns = right.shape[1] // 3
    r = width // 32
    wide = columns + out_keep.shape[1] // 2

    def whole(shape):
        return spec(shape, lambda j, p: (0,) * len(shape))

    shapes = [(2, 4, r, wide)] * 2 + [(4, 2, r, wide)] * 2 + [(2, 2, 2, r, columns)] * 2
    return pl.pallas_call(
        inner_keep_kernel,
        grid_spec=pltpu.PrefetchScalarGridSpec(
            num_scalar_prefetch=1,
            grid=(3,),
            in_specs=[
                ANY,
                whole((2, 2, width // 4, rows)),
                spec((rows, columns), lambda j, p: (0, j)),
                spec((1, width // 2, columns), lambda j, p: (j, 0, 0)),
                whole(out_keep.shape),
                whole(out_keep.shape),
            ],
            out_specs=[whole(s) for s in shapes] + [whole((8, 128))],
        ),
        out_shape=[jax.ShapeDtypeStruct(s, single) for s in shapes] + [TOKEN],
        compiler_params=params(),
        cost_estimate=cost(10e9),
        name="inner_weight_keep",
    )(pos, token, left_t.reshape(2, 2, width // 4, rows), right, got, out_keep, out_got)


def qkv_send_kernel(pos_ref, left_ref, dq_ref, dk_ref, dv_ref, send_ref, tok_ref, *, other):
    me = 1 - pos_ref[1] if other else pos_ref[1]
    left = row_half(left_ref, me)
    for t, ref in enumerate((dq_ref, dk_ref, dv_ref)):
        send_ref[t] = dot(left, ref[...])
    tok_ref[...] = send_ref[0, 0:8, 0:128]


def qkv_send(pos, xt, dq, dk, dv, other):
    width, rows = xt.shape

    def whole(shape):
        return spec(shape, lambda j, p: (0,) * len(shape))

    return pl.pallas_call(
        functools.partial(qkv_send_kernel, other=other),
        grid_spec=pltpu.PrefetchScalarGridSpec(
            num_scalar_prefetch=1,
            grid=(1,),
            in_specs=[whole((2, 2, width // 4, rows))] + [whole((rows, width))] * 3,
            out_specs=[whole((3, width // 2, width)), whole((8, 128))],
        ),
        out_shape=[jax.ShapeDtypeStruct((3, width // 2, width), single), TOKEN],
        compiler_params=params(),
        cost_estimate=cost(10e9),
        name="qkv_weight_send",
    )(pos, xt.reshape(2, 2, width // 4, rows), dq, dk, dv)


def qkv_keep_kernel(pos_ref, token_ref, left_ref, dq_ref, dk_ref, dv_ref, got_ref, sx_ref, kx_ref, sy_ref, ky_ref, tok_ref):
    left = row_half(left_ref, pos_ref[1])
    width = dq_ref.shape[1]
    mid = width // 2
    rows = width // 32
    gq, gk, gv = [dot(left, ref[...]) + got_ref[t] for t, ref in enumerate((dq_ref, dk_ref, dv_ref))]
    tok_ref[...] = gq[0:8, 0:128]
    for y in range(2):
        sub = slice(y * 8 * rows, (y + 1) * 8 * rows)
        split_x(pos_ref, gq[sub], rows, slice(None), (y,), sx_ref, kx_ref, slice(0, width))
        split_x(pos_ref, gk[sub], rows, slice(0, mid), (y,), sx_ref, kx_ref, slice(width, width + mid))
    me = pos_ref[0]
    for data, to in ((gk[:, mid:], slice(0, mid)), (gv, slice(mid, mid + width))):
        zero = data[: 8 * rows].reshape(4, 2, rows, data.shape[1])
        one = data[8 * rows :].reshape(4, 2, rows, data.shape[1])
        sy_ref[:, :, :, to] = jnp.where(me == 0, one, zero)
        ky_ref[:, :, :, to] = jnp.where(me == 0, zero, one)


def qkv_keep(pos, token, xt, dq, dk, dv, got):
    width, rows = xt.shape
    r = width // 32
    wide = width + width // 2

    def whole(shape):
        return spec(shape, lambda j, p: (0,) * len(shape))

    shapes = [(2, 4, r, wide)] * 2 + [(4, 2, r, wide)] * 2
    return pl.pallas_call(
        qkv_keep_kernel,
        grid_spec=pltpu.PrefetchScalarGridSpec(
            num_scalar_prefetch=1,
            grid=(1,),
            in_specs=[ANY, whole((2, 2, width // 4, rows))] + [whole((rows, width))] * 3 + [whole((3, width // 2, width))],
            out_specs=[whole(s) for s in shapes] + [whole((8, 128))],
        ),
        out_shape=[jax.ShapeDtypeStruct(s, single) for s in shapes] + [TOKEN],
        compiler_params=params(),
        cost_estimate=cost(10e9),
        name="qkv_weight_keep",
    )(pos, token, xt.reshape(2, 2, width // 4, rows), dq, dk, dv, got)


def token_grad_kernel(token_ref, dr1_ref, dq_ref, dk_ref, dv_ref, wq_ref, wk_ref, wv_ref, out_ref):
    out_ref[...] = (
        dr1_ref[...]
        + dot(dq_ref[...], wq_ref[...], NT)
        + dot(dk_ref[...], wk_ref[...], NT)
        + dot(dv_ref[...], wv_ref[...], NT)
    )


def token_grads(token, dr1, dq, dk, dv, wq, wk, wv):
    rows, width = dr1.shape
    tile = spec((TILE, width), lambda i: (i, 0))
    w = spec((width, width), lambda i: (0, 0))
    return pl.pallas_call(
        token_grad_kernel,
        grid=(rows // TILE,),
        in_specs=[ANY, tile, tile, tile, tile, w, w, w],
        out_specs=tile,
        out_shape=jax.ShapeDtypeStruct((rows, width), single),
        compiler_params=params(),
        cost_estimate=cost(10e9),
        name="token_grad",
    )(token, dr1, dq, dk, dv, wq, wk, wv)


def pair_list(change):
    pairs = []
    for y in range(2):
        for c in range(2):
            for z in range(4):
                for x in range(2):
                    py, pc, pz, px = change(y, c, z, x)
                    pairs.append((((y * 2 + c) * 4 + z) * 2 + x, ((py * 2 + pc) * 4 + pz) * 2 + px))
    return pairs


PAIRS = {
    "y": pair_list(lambda y, c, z, x: (1 - y, c, z, x)),
    "c": pair_list(lambda y, c, z, x: (y, 1 - c, z, x)),
    "x": pair_list(lambda y, c, z, x: (y, c, z, 1 - x)),
    "near": pair_list(lambda y, c, z, x: (y, c, z ^ 1, x)),
    "far": pair_list(lambda y, c, z, x: (y, c, 3 - z, x)),
}


def swap(array, name):
    return lax.ppermute(array, ALL_AXES, PAIRS[name])


def take(array, axis, index):
    return lax.dynamic_index_in_dim(array, index, axis, keepdims=False)


def halves(parts, axis, me):
    return sum_of([take(p, axis, 1 - me) for p in parts]), [take(p, axis, me) for p in parts]


def sum_of(parts):
    return functools.reduce(jnp.add, parts)


def z_sides(parts, side):
    zero = [jnp.stack([p[0], p[3]]) for p in parts]
    one = [jnp.stack([p[1], p[2]]) for p in parts]
    sent = sum_of([jnp.where(side == 0, b, a) for a, b in zip(zero, one)])
    kept = [jnp.where(side == 0, a, b) for a, b in zip(zero, one)]
    return sent, kept


def small_sum(array):
    for name in ("c", "x", "y", "near", "far"):
        array = array + swap(array, name)
    return array


def per_device(
    tokens,
    out_cot,
    lengths,
    labels,
    task_ids,
    task_weights,
    query_weight,
    key_weight,
    value_weight,
    query_bias,
    value_bias,
    output_weight,
    output_bias,
    norm1_gain,
    norm1_bias,
    inner_weight,
    inner_bias,
    outer_weight,
    outer_bias,
    norm2_gain,
    norm2_bias,
    head_table,
    *,
    staged,
):
    seqs, length, width = tokens.shape
    rows = seqs * length
    ff = inner_weight.shape[1]
    group_seqs = seqs * lax.axis_size("batch")
    task_index = lax.axis_index("task")
    batch_index = lax.axis_index("batch")
    my_y, my_c, my_z, my_x = task_index // 2, task_index % 2, batch_index // 2, batch_index % 2
    my_hi = my_z // 2
    my_side = (my_z // 2) ^ (my_z % 2)
    pos = jnp.stack([my_y, my_c, my_x, my_side, my_hi]).astype(jnp.int32)
    vec = jnp.stack(
        [output_bias, norm1_gain, norm1_bias, outer_bias, norm2_gain, norm2_bias, norm2_bias, norm2_bias]
    ).astype(single)

    q, k, v, ctx, ctxt, lse = attention(
        tokens, lengths, query_weight, key_weight, value_weight, query_bias, value_bias
    )
    block_out, normed1, root1, h1t, act, slope, dr2, ddown, sums2 = middle(
        tokens,
        ctx,
        out_cot,
        labels,
        task_ids,
        task_weights,
        output_weight,
        inner_weight,
        outer_weight,
        vec,
        inner_bias,
        head_table,
        group_seqs,
    )
    block_out = block_out.reshape(tokens.shape)
    x_rows = tokens.reshape(rows, width)

    o_send = outer_send(pos, act, ddown, True)
    if staged:
        o_got = swap(o_send, "c")
    dinner, inner_bias_sum = inner_grad(o_send, ddown, outer_weight, slope)
    if staged:
        osx, okx, osy, oky, osz, okz, token = outer_keep(pos, dinner, act, ddown, o_got)
        orx, ory, orz = swap(osx, "x"), swap(osy, "y"), swap(osz, "near")
    else:
        o_keep = outer_send(pos, act, ddown, False)
        token = o_keep
    i_send, token = rows_send(pos, token, h1t, dinner, True, 3)
    if staged:
        i_got = swap(i_send, "c")
    dr1, dctx, xt, out_send, out_keep, sums1 = first_norm(
        pos, token, dinner, inner_weight, dr2, normed1, root1, output_weight, ctxt, vec, x_rows
    )
    if staged:
        out_got = swap(out_send, "c")
        isx, ikx, isy, iky, isz, ikz, token = inner_keep(pos, dr1, h1t, dinner, i_got, out_keep, out_got)
        irx, iry, irz = swap(isx, "x"), swap(isy, "y"), swap(isz, "near")
    else:
        i_keep, token = rows_send(pos, token, h1t, dinner, False, 3)
    dq, dk, dv, sums0 = attention_back(lengths, token, q, k, v, ctx, dctx, lse)
    dq, dk, dv = [a.reshape(rows, width) for a in (dq, dk, dv)]
    qkv_s, token = qkv_send(pos, xt, dq, dk, dv, True)

    if staged:
        qkv_got = swap(qkv_s, "c")

        def second(kx, rx, ky, ry, kz, rz):
            xs, xk = halves([kx, rx], 0, my_y)
            ys, yk = halves([ky, ry], 1, my_x)
            xk.append(swap(xs, "y"))
            yk.append(swap(ys, "x"))
            if kz is None:
                return xk, yk, None
            zs, zk = halves([kz, rz], 1, my_hi)
            zk.append(swap(zs, "far"))
            return xk, yk, zk

        def third(xk, yk, zk):
            xs, xk = z_sides(xk, my_side)
            ys, yk = z_sides(yk, my_side)
            got = swap(jnp.concatenate([xs, ys], axis=-1), "near")
            split = xs.shape[-1]
            xk.append(got[..., :split])
            yk.append(got[..., split:])
            if zk is None:
                return xk, yk, None
            zs, zk = halves(zk, 1, my_x)
            zk.append(swap(zs, "x"))
            return xk, yk, zk

        def fourth(xk, yk, zk):
            xs, xk = halves(xk, 0, my_hi)
            ys, yk = halves(yk, 0, my_hi)
            got = swap(jnp.concatenate([xs, ys], axis=-1), "far")
            split = xs.shape[-1]
            x_sum = sum_of(xk + [got[..., :split]])
            y_sum = sum_of(yk + [got[..., split:]])
            if zk is None:
                return x_sum, y_sum, None
            zs, zk = halves(zk, 0, my_y)
            return x_sum, y_sum, sum_of(zk + [swap(zs, "y")])

        o_parts = fourth(*third(*second(okx, orx, oky, ory, okz, orz)))
        i_parts = fourth(*third(*second(ikx, irx, iky, iry, ikz, irz)))
    token_grad = token_grads(token, dr1, dq, dk, dv, query_weight, key_weight, value_weight)
    token_grad = token_grad.reshape(tokens.shape)

    classes = head_table.shape[1]
    chooser = (jnp.arange(head_table.shape[0], dtype=jnp.int32) == task_ids[0]).astype(single)
    head_local = (chooser[:, None, None] * sums2[None, 3 : 3 + classes, :]).reshape(-1, width)
    loss_row = jnp.where(jnp.arange(width)[None, :] == task_index, sums2[7:8], 0.0)
    bias0 = sums0.sum(axis=0).transpose(1, 0, 2).reshape(8, width)
    small = jnp.concatenate(
        [bias0[:2], sums1[:3], inner_bias_sum.reshape(-1, width), sums2[:3], loss_row, head_local], axis=0
    )

    if staged:
        small = small_sum(small)
        qsx, qkx, qsy, qky, token = qkv_keep(pos, token_grad, xt, dq, dk, dv, qkv_got)
        qrx, qry = swap(qsx, "x"), swap(qsy, "y")
        q_x, q_y, _ = fourth(*third(*second(qkx, qrx, qky, qry, None, None)))
        mid = width // 2
        wide = i_parts[2].shape[-1]
        outer_s = jnp.concatenate(o_parts, axis=-1)
        inner_s = jnp.concatenate([i_parts[0][:, :wide], i_parts[1][:, :wide], i_parts[2]], axis=-1)
        output_s = jnp.concatenate([i_parts[0][:, wide:], i_parts[1][:, wide:]], axis=-1)
        query_s = q_x[:, :width]
        key_s = jnp.concatenate([q_x[:, width:], q_y[:, :mid]], axis=-1)
        value_s = q_y[:, mid:]
    else:
        small = lax.psum(small, ALL_AXES)
        qkv_k, _ = qkv_send(pos, xt, dq, dk, dv, False)

        def whole_rows(sent, kept):
            both = jnp.stack([jnp.where(my_c == 0, kept, sent), jnp.where(my_c == 0, sent, kept)], axis=1)
            return both.reshape(-1, both.shape[-1])

        def scatter(grad):
            return lax.psum_scatter(grad, ALL_AXES, scatter_dimension=0, tiled=True)

        def by_rows(array):
            return array.reshape(2, -1, array.shape[-1])

        outer_s = scatter(whole_rows(o_send, o_keep))
        inner_s = scatter(
            jnp.concatenate([whole_rows(by_rows(i_send[j]), by_rows(i_keep[j])) for j in range(3)], axis=-1)
        )
        output_s = scatter(whole_rows(by_rows(out_send), by_rows(out_keep)))
        query_s, key_s, value_s = [scatter(whole_rows(by_rows(qkv_s[t]), by_rows(qkv_k[t]))) for t in range(3)]

    where = task_index * lax.axis_size("batch") + batch_index
    devices = lax.axis_size("task") * lax.axis_size("batch")

    def mine(array):
        flat = array.reshape(-1)
        count = flat.shape[0] // devices
        return lax.dynamic_slice(flat, (where * count,), (count,))

    bias_rows = ff // width
    at = 5 + bias_rows
    loss = lax.dynamic_slice(small, (at + 3, task_index), (1, 1)).reshape(1)
    head_grad = small[at + 4 :].reshape(head_table.shape)
    return (
        block_out,
        token_grad,
        loss,
        query_s,
        key_s,
        value_s,
        mine(small[0]),
        mine(small[1]),
        output_s,
        mine(small[4]),
        mine(small[2]),
        mine(small[3]),
        inner_s,
        mine(small[5:at]),
        outer_s,
        mine(small[at + 2]),
        mine(small[at]),
        mine(small[at + 1]),
        head_grad,
    )


def solution(mesh):
    rows = P(ALL_AXES)
    plain = P()
    task = P("task")
    staged = mesh.shape["task"] == 4 and mesh.shape["batch"] == 8
    return jax.shard_map(
        functools.partial(per_device, staged=staged),
        mesh=mesh,
        in_specs=(rows, rows, rows, rows, task, task) + (plain,) * 16,
        out_specs=(rows, rows, task) + (rows,) * 15 + (plain,),
        check_vma=False,
    )
```

time: 935 us -> 353 us (0.38)
  waiting for transfers between devices: 596 us -> 98.4 us
  matrix products: 163 us -> 0 us
  Pallas kernels: 0 us -> 152 us
  blocking collectives: 61.9 us -> 0 us
  starting transfers between devices: 0.54 us -> 46.3 us
  other arithmetic: 34.5 us -> 12.8 us
  between operations: 18.5 us -> 2.69 us
  local copies, waits for them, and re-layouts: 53.1 us -> 39.5 us
    unnamed x10 -> x0, waiting for transfers between devices: 313 us -> none
    reduce_scatter x3 -> x0, waiting for transfers between devices: 283 us -> none  [the longest x1 142 us: per_device(): lax.psum_scatter(inner_weight_local, ('task', 'batch'), scatter_dimension...]
    pallas_call x0 -> x12, Pallas kernels: none -> 152 us  [the longest x1 27.1 us: middle(): pl.pallas_call(functools.partial(middle_kernel, tiles_per_seq=length // T...]
    dot_general x27 -> x0, matrix products: 147 us -> none  [the longest x6 32.9 us: product_tn(): lax.dot_general(left, right, (((0,), (0,)), ((), ())), preferred_element_...]
    ppermute x0 -> x35, waiting for transfers between devices: none -> 98.4 us  [swap(): return lax.ppermute(array, ALL_AXES, PAIRS[name])]
    ppermute x0 -> x35, starting transfers between devices: none -> 46.3 us  [swap(): return lax.ppermute(array, ALL_AXES, PAIRS[name])]
    unnamed x1 -> x0, blocking collectives: 38.2 us -> none
    psum x1 -> x0, blocking collectives: 23.7 us -> none  [per_device(): loss_total = lax.psum(jnp.sum(losses), 'batch')]
  transfers between devices with their start and end apart: 7 -> 35, of which waited for: 5 -> 18; matrix products, arithmetic and copies ran while one was open for 17% -> 7% of each run, Pallas kernels for 0% -> 16%
where the time goes in v1:
time: 353 us; the launch traced here: 351 us
  Pallas kernels  152 us (43%)
  waiting for transfers between devices  98.4 us (28%)
  starting transfers between devices  46.3 us (13%)
  local copies, waits for them, and re-layouts  39.5 us (11%)
  other arithmetic  12.8 us (4%)
    ppermute x35, waiting for transfers between devices, swap(): return lax.ppermute(array, ALL_AXES, PAIRS[name])  98.4 us
    ppermute x35, starting transfers between devices, swap(): return lax.ppermute(array, ALL_AXES, PAIRS[name])  46.3 us
    pallas_call x1, Pallas kernels, middle(): pl.pallas_call(functools.partial(middle_kernel, tiles_per_seq=length // T...  27.1 us
    pallas_call x1, Pallas kernels, first_norm(): pl.pallas_call(first_norm_kernel, grid_spec=pltpu.PrefetchScalarGridSpec(...  20.5 us
    pallas_call x1, Pallas kernels, attention_back(): pl.pallas_call(attention_back_kernel, grid_spec=pltpu.PrefetchScalarGridS...  20.4 us
    unnamed x62, local copies, waits for them, and re-layouts  17.2 us
    pallas_call x1, Pallas kernels, attention(): pl.pallas_call(attention_kernel, grid_spec=pltpu.PrefetchScalarGridSpec(n...  14.4 us
    pallas_call x1, Pallas kernels, inner_keep(): pl.pallas_call(inner_keep_kernel, grid_spec=pltpu.PrefetchScalarGridSpec(...  10.7 us
  transfers between devices with their start and end apart: 35, of which 18 were waited for; matrix products, arithmetic and copies ran while one was open for 7% of the time, Pallas kernels for 16%

profile of v1, /device:TPU:0, one launch (start us, length us, event | category | flops | bytes accessed | tf_op | source)
XLA Modules:
  0.0 351.2 jit_solution(6647753903211490729)
XLA Ops:
  17.4 14.4 %attention_forward.1 = (bf16[2,512,768]{2,1,0:T(8,128)(2,1)S(1)}, bf16[2,512,768]{2,1,0:T(8,128)(2,1)S(1)}, bf16[2,512,768]{2,1,0:T(8,128)(2,1)S(1)}, bf16[2,512...) custom-call(s32[2]{0:T(128)S(1)} %copy-done.4, ...), custom_call_target="tpu_custom_call" | custom-call | flops 15000000512 | bytes 1048576 | tf_op jit(solution)/shard_map/attention_forward/pallas_call | solution.py:91
  38.4 27.1 %middle_forward.1 = (bf16[1024,768]{1,0:T(8,128)(2,1)}, f32[1024,768]{1,0:T(8,128)}, f32[1024,128]{1,0:T(8,128)}, bf16[768,1024]{1,0:T(8,128)(2,1)}, bf16[1024,3...) custom-call(s32[1]{0:T(128)} %copy.80.task_ref, ...), custom_call_target="tpu_custom_call" | custom-call | flops 20000000000 | bytes 1048576 | tf_op jit(solution)/shard_map/middle_forward/pallas_call | solution.py:239
  65.5 6.9 %outer_weight_send.1.token_ref = f32[2,768,768]{2,1,0:T(8,128)} custom-call(s32[5]{0:T(128)} %stack.161.pos_ref, bf16[1024,3072]{1,0:T(8,128)(2,1)} %get-tuple-element.70.act_ref, bf16[1024,768]{1,0:T(8,128)(2,1)} %get-tuple-element.71.ddown_ref), custom_call_target="tpu_custom_call" | custom-call | flops 10000000000 | bytes 1048576 | tf_op jit(solution)/shard_map/outer_weight_send/pallas_call | solution.py:486
  72.9 10.7 %inner_grad.1 = (bf16[1024,3072]{1,0:T(8,128)(2,1)}, f32[1,3072]{1,0:T(1,128)}) custom-call(f32[2,768,768]{2,1,0:T(8,128)} %outer_weight_send.1.token_ref, bf16[1024,768]{1,0:T(8,128)(2,1)} %get-tuple-element.71.ddown_ref, bf16[3072,768]{1,0:T(8,128)(2,1)} %wd_ref.3, bf16[1024,3072]{1,0:T(8,128)(2,1)} %get-tuple-element.72.slope_ref), custom_call_target="tpu_custom_call" | custom-call | flops 20000000000 | bytes 1048576 | tf_op jit(solution)/shard_map/inner_grad/pallas_call | solution.py:309
  85.9 8.0 %outer_weight_keep.1 = (f32[2,4,96,256]{3,2,1,0:T(8,128)}, f32[2,4,96,256]{3,2,1,0:T(8,128)}, f32[4,2,96,256]{3,2,1,0:T(8,128)}, f32[4,2,96,256]{3,2,1,0:T(8,128...) custom-call(s32[5]{0:T(128)} %stack.161.pos_ref, ...), custom_call_target="tpu_custom_call" | custom-call | flops 10000000000 | bytes 1048576 | tf_op jit(solution)/shard_map/outer_weight_keep/pallas_call | solution.py:550
  93.9 8.6 %weight_rows_send.1 = (f32[3,384,1024]{2,1,0:T(8,128)}, f32[8,128]{1,0:T(8,128)}) custom-call(s32[5]{0:T(128)} %stack.161.pos_ref, f32[8,128]{1,0:T(8,128)} %get-tuple-element.74.token_ref, bf16[2,2,192,1024]{3,2,1,0:T(8,128)(2,1)} %bitcast.232, bf16[1024,3072]{1,0:T(8,128)(2,1)} %get-tuple-element.73.token_ref.right_ref.dinner_ref), custom_call_target="tpu_custom_call" | custom-call | flops 10000000000 | bytes 1048576 | tf_op jit(solution)/shard_map/weight_rows_send/pallas_call | solution.py:586
  102.6 2.9 collective-permute-start.25
  108.7 20.5 %first_norm_back.1 = (f32[1024,768]{1,0:T(8,128)}, bf16[1024,768]{1,0:T(8,128)(2,1)}, bf16[768,1024]{1,0:T(8,128)(2,1)}, f32[384,768]{1,0:T(8,128)}, f32[384,768]{1,0:T(8,128)}, /*index=5*/f32[8,768]{1,0:T(8,128)}) custom-call(s32[5]{0:T(128)} %stack.161.pos_ref, f32[8,128]{1,0:T(8,128)} %get-tuple-element.76.token_ref, ...), custom_call_target="tpu_custom_call" | custom-call | flops 20000000000 | bytes 1048576 | tf_op jit(solution)/shard_map/first_norm_back/pallas_call | solution.py:382
  131.6 2.5 collective-permute-start.32
  134.2 7.6 %collective-permute-done.26 = f32[4,96,256]{2,1,0:T(8,128)S(1)} collective-permute-done((f32[4,96,256]{2,1,0:T(8,128)S(1)}, f32[4,96,256]{2,1,0:T(8,128)S(1)}, u32[]{:S(2)}, u32[]{:S(2)}) %collective-permute-start.26) | collective-permute-done | bytes 393248 | tf_op jit(solution)/shard_map/ppermute | solution.py:806
  146.3 4.8 %collective-permute-done.33 = f32[2,96,256]{2,1,0:T(8,128)S(1)} collective-permute-done((f32[2,96,256]{2,1,0:T(8,128)S(1)}, f32[2,96,256]{2,1,0:T(8,128)S(1)}, u32[]{:S(2)}, u32[]{:S(2)}) %collective-permute-start.33) | collective-permute-done | bytes 196640 | tf_op jit(solution)/shard_map/ppermute | solution.py:806
  153.4 2.6 collective-permute-start.30
  156.0 4.9 %collective-permute-done.30 = f32[96,512]{1,0:T(8,128)S(1)} collective-permute-done((f32[96,512]{1,0:T(8,128)S(1)}, f32[96,512]{1,0:T(8,128)S(1)}, u32[]{:S(2)}, u32[]{:S(2)}) %collective-permute-start.30) | collective-permute-done | bytes 196640 | tf_op jit(solution)/shard_map/ppermute | solution.py:806
  162.0 10.7 %inner_weight_keep.1 = (f32[2,4,24,1408]{3,2,1,0:T(8,128)}, f32[2,4,24,1408]{3,2,1,0:T(8,128)}, f32[4,2,24,1408]{3,2,1,0:T(8,128)}, f32[4,2,24,1408]{3,2,1,0:T(8...) custom-call(s32[5]{0:T(128)} %stack.161.pos_ref, ...), custom_call_target="tpu_custom_call" | custom-call | flops 10000000000 | bytes 1048576 | tf_op jit(solution)/shard_map/inner_weight_keep/pallas_call | solution.py:666
  172.8 20.4 %attention_back.1 = (bf16[2,512,768]{2,1,0:T(8,128)(2,1)}, bf16[2,512,768]{2,1,0:T(8,128)(2,1)}, bf16[2,512,768]{2,1,0:T(8,128)(2,1)}, f32[2,3,8,256]{3,2,1,0:T(8,128)}) custom-call(s32[2]{0:T(128)} %n_ref.3, f32[8,128]{1,0:T(8,128)} %get-tuple-element.86.token_ref, bf16[2,512,768]{2,1,0:T(8,128)(2,1)} %copy-done.6, bf16[2,512,768]{2,1,0:T(8,128)(2,1)} %copy-done.7, ...), custom_call_target="tpu_custom_call" | custom-call | flops 20000000000 | bytes 1048576 | tf_op jit(solution)/shard_map/attention_back/pallas_call | solution.py:462
  195.1 5.3 %collective-permute-start.21 = (f32[2,2,2,24,1024]{4,3,2,1,0:T(8,128)}, f32[2,2,2,24,1024]{4,3,2,1,0:T(8,128)}, u32[]{:S(2)}, u32[]{:S(2)}) collective-permute-start(f32[2,2,2,24,1024]{4,3,2,1,0:T(8,128)} %get-tuple-element.110), channel_id=1, source_target_pairs={{0,2},{1,3},{2,0},{3,1},{4,6},{5,7},{6,4},{7,5},{8,10},{9,11},{10,... | collective-permute-start | bytes 2359304 | tf_op jit(solution)/shard_map/ppermute | solution.py:806
  204.8 7.3 %qkv_weight_send.1 = (f32[3,384,768]{2,1,0:T(8,128)}, f32[8,128]{1,0:T(8,128)}) custom-call(s32[5]{0:T(128)} %stack.161.pos_ref, bf16[2,2,192,1024]{3,2,1,0:T(8,128)(2,1)} %bitcast.230, bf16[1024,768]{1,0:T(8,128)(2,1)} %bitcast.234, bf16[1024,768]{1,0:T(8,128)(2,1)} %bitcast.237, bf16[1024,768]{1,0:T(8,128)(2,1)} %bitcast.240), custom_call_target="tpu_custom_call" | custom-call | flops 10000000000 | bytes 1048576 | tf_op jit(solution)/shard_map/qkv_weight_send/pallas_call | solution.py:702
  212.1 17.1 %collective-permute-done.4 = f32[37,768]{1,0:T(8,128)S(1)} collective-permute-done((f32[37,768]{1,0:T(8,128)S(1)}, f32[37,768]{1,0:T(8,128)S(1)}, u32[]{:S(2)}, u32[]{:S(2)}) %collective-permute-start.4) | collective-permute-done | bytes 113696 | tf_op jit(solution)/shard_map/ppermute | solution.py:806
  230.5 9.0 %token_grad.1 = f32[1024,768]{1,0:T(8,128)} custom-call(f32[8,128]{1,0:T(8,128)} %get-tuple-element.95.token_ref, f32[1024,768]{1,0:T(8,128)} %get-tuple-element.82.token_ref.dr1_ref, bf16[1024,768]{1,0:T(8,128)(2,1)} %bitcast.235, bf16[1024,768]{1,0:T(8,128)(2,1)} %bitcast.238, bf16[1024,768]{1,0:T(8,128)(2,1)} %bitcast.241, bf16[768,768]{1,0:T(8,128)(2,1)} %wq_ref.3, ...), custom_call_target="tpu_custom_call" | custom-call | flops 10000000000 | bytes 1048576 | tf_op jit(solution)/shard_map/token_grad/pallas_call | solution.py:773
  240.7 3.8 %collective-permute-done.6 = f32[37,768]{1,0:T(8,128)S(1)} collective-permute-done((f32[37,768]{1,0:T(8,128)S(1)}, f32[37,768]{1,0:T(8,128)S(1)}, u32[]{:S(2)}, u32[]{:S(2)}) %collective-permute-start.6) | collective-permute-done | bytes 113696 | tf_op jit(solution)/shard_map/ppermute | solution.py:806
  244.5 2.4 collective-permute-start.7
  247.6 3.6 %collective-permute-done.7 = f32[37,768]{1,0:T(8,128)S(1)} collective-permute-done((f32[37,768]{1,0:T(8,128)S(1)}, f32[37,768]{1,0:T(8,128)S(1)}, u32[]{:S(2)}, u32[]{:S(2)}) %collective-permute-start.7) | collective-permute-done | bytes 113696 | tf_op jit(solution)/shard_map/ppermute | solution.py:806
  268.9 2.4 collective-permute-done.22
  274.0 6.9 %collective-permute-done.23 = f32[2,24,1024]{2,1,0:T(8,128)S(1)} collective-permute-done((f32[2,24,1024]{2,1,0:T(8,128)S(1)}, f32[2,24,1024]{2,1,0:T(8,128)S(1)}, u32[]{:S(2)}, u32[]{:S(2)}) %collective-permute-start.23) | collective-permute-done | bytes 196640 | tf_op jit(solution)/shard_map/ppermute | solution.py:806
  282.9 3.5 collective-permute-done.24
  288.6 3.2 collective-permute-start.19
  291.8 7.8 %qkv_weight_keep.1 = (f32[2,4,24,1152]{3,2,1,0:T(8,128)}, f32[2,4,24,1152]{3,2,1,0:T(8,128)}, f32[4,2,24,1152]{3,2,1,0:T(8,128)}, f32[4,2,24,1152]{3,2,1,0:T(8,128)}, f32[8,128]{1,0:T(8,128)}) custom-call(s32[5]{0:T(128)} %stack.161.pos_ref, f32[2,512,768]{2,1,0:T(8,128)} %bitcast.227, bf16[2,2,192,1024]{3,2,1,0:T(8,128)(2,1)} %bitcast.231, ...), custom_call_target="tpu_custom_call" | custom-call | flops 10000000000 | bytes 1048576 | tf_op jit(solution)/shard_map/qkv_weight_keep/pallas_call | solution.py:745
  304.2 14.3 %collective-permute-done.9 = f32[2,4,24,1152]{3,2,1,0:T(8,128)S(1)} collective-permute-done((f32[2,4,24,1152]{3,2,1,0:T(8,128)}, f32[2,4,24,1152]{3,2,1,0:T(8,128)S(1)}, u32[]{:S(2)}, u32[]{:S(2)}) %collective-permute-start.9) | collective-permute-done | bytes 884768 | tf_op jit(solution)/shard_map/ppermute | solution.py:806
  322.1 4.8 %collective-permute-done.10 = f32[4,24,1152]{2,1,0:T(8,128)S(1)} collective-permute-done((f32[4,24,1152]{2,1,0:T(8,128)S(1)}, f32[4,24,1152]{2,1,0:T(8,128)S(1)}, u32[]{:S(2)}, u32[]{:S(2)}) %collective-permute-start.10) | collective-permute-done | bytes 442400 | tf_op jit(solution)/shard_map/ppermute | solution.py:806
  326.9 3.4 collective-permute-done.12
  331.2 10.1 %collective-permute-done.13 = f32[2,24,2304]{2,1,0:T(8,128)S(1)} collective-permute-done((f32[2,24,2304]{2,1,0:T(8,128)S(1)}, f32[2,24,2304]{2,1,0:T(8,128)S(1)}, u32[]{:S(2)}, u32[]{:S(2)}) %collective-permute-start.13) | collective-permute-done | bytes 442400 | tf_op jit(solution)/shard_map/ppermute | solution.py:806
  343.9 5.3 %collective-permute-done.14 = f32[24,2304]{1,0:T(8,128)S(1)} collective-permute-done((f32[24,2304]{1,0:T(8,128)S(1)}, f32[24,2304]{1,0:T(8,128)S(1)}, u32[]{:S(2)}, u32[]{:S(2)}) %collective-permute-start.14) | collective-permute-done | bytes 221216 | tf_op jit(solution)/shard_map/ppermute | solution.py:806
  (229 shorter events, 85.4 us)
Async XLA Ops:
  72.4 13.5 %collective-permute-start = (f32[2,768,768]{2,1,0:T(8,128)}, f32[2,768,768]{2,1,0:T(8,128)}, u32[]{:S(2)}, u32[]{:S(2)}) collective-permute-start(f32[2,768,768]{2,1,0:T(8,128)} %outer_weight_send.1.token_ref), channel_id=1, source_target_pairs={{0,8},{1,9},{2,10},{3,11},{4,12},{5,13},{6,14},{7,15},{8,0},{9,1},... | collective-permute-start | bytes 14155784 | tf_op jit(solution)/shard_map/ppermute | solution.py:806
  102.5 58.5 %collective-permute-start.1 = (f32[3,384,1024]{2,1,0:T(8,128)}, f32[3,384,1024]{2,1,0:T(8,128)}, u32[]{:S(2)}, u32[]{:S(2)}) collective-permute-start(f32[3,384,1024]{2,1,0:T(8,128)} %get-tuple-element.83), channel_id=1, source_target_pairs={{0,8},{1,9},{2,10},{3,11},{4,12},{5,13},{6,14},{7,15},{8,0},{9,1},... | collective-permute-start | bytes 14155784 | tf_op jit(solution)/shard_map/ppermute | solution.py:806
  102.6 27.6 %collective-permute-start.25 = (f32[2,4,96,256]{3,2,1,0:T(8,128)}, f32[2,4,96,256]{3,2,1,0:T(8,128)S(1)}, u32[]{:S(2)}, u32[]{:S(2)}) collective-permute-start(f32[2,4,96,256]{3,2,1,0:T(8,128)} %get-tuple-element.112), channel_id=1, source_target_pairs={{0,1},{1,0},{2,3},{3,2},{4,5},{5,4},{6,7},{7,6},{8,9},{9,8},{10,11... | collective-permute-start | bytes 2359304 | tf_op jit(solution)/shard_map/ppermute | solution.py:806
  105.6 25.3 %collective-permute-start.27 = (f32[4,2,96,256]{3,2,0,1:T(8,128)S(1)}, f32[4,2,96,256]{3,2,0,1:T(8,128)S(1)}, u32[]{:S(2)}, u32[]{:S(2)}) collective-permute-start(f32[4,2,96,256]{3,2,0,1:T(8,128)S(1)} %copy.70), channel_id=1, source_target_pairs={{0,16},{1,17},{2,18},{3,19},{4,20},{5,21},{6,22},{7,23},{8,24},{9,... | collective-permute-start | bytes 2359304 | tf_op jit(solution)/shard_map/ppermute | solution.py:806
  107.2 24.4 %collective-permute-start.31 = (f32[2,2,2,96,256]{4,3,2,1,0:T(8,128)}, f32[2,2,2,96,256]{4,3,2,1,0:T(8,128)S(1)}, u32[]{:S(2)}, u32[]{:S(2)}) collective-permute-start(f32[2,2,2,96,256]{4,3,2,1,0:T(8,128)} %get-tuple-element.116), channel_id=1, source_target_pairs={{0,2},{1,3},{2,0},{3,1},{4,6},{5,7},{6,4},{7,5},{8,10},{9,11},{10,... | collective-permute-start | bytes 2359304 | tf_op jit(solution)/shard_map/ppermute | solution.py:806
  129.3 31.7 %collective-permute-start.2 = (f32[384,768]{1,0:T(8,128)}, f32[384,768]{1,0:T(8,128)S(1)}, u32[]{:S(2)}, u32[]{:S(2)}) collective-permute-start(f32[384,768]{1,0:T(8,128)} %get-tuple-element.85), channel_id=1, source_target_pairs={{0,8},{1,9},{2,10},{3,11},{4,12},{5,13},{6,14},{7,15},{8,0},{9,1},... | collective-permute-start | bytes 3538952 | tf_op jit(solution)/shard_map/ppermute | solution.py:806
  130.3 11.6 %collective-permute-start.26 = (f32[4,96,256]{2,1,0:T(8,128)S(1)}, f32[4,96,256]{2,1,0:T(8,128)S(1)}, u32[]{:S(2)}, u32[]{:S(2)}) collective-permute-start(f32[4,96,256]{2,1,0:T(8,128)S(1)} %add_bitcast_fusion.6), channel_id=1, source_target_pairs={{0,16},{1,17},{2,18},{3,19},{4,20},{5,21},{6,22},{7,23},{8,24},{9,... | collective-permute-start | bytes 1179656 | tf_op jit(solution)/shard_map/ppermute | solution.py:806
  131.0 11.3 %collective-permute-start.28 = (f32[4,96,256]{2,1,0:T(8,128)S(1)}, f32[4,96,256]{2,1,0:T(8,128)S(1)}, u32[]{:S(2)}, u32[]{:S(2)}) collective-permute-start(f32[4,96,256]{2,1,0:T(8,128)S(1)} %get-tuple-element.202), channel_id=1, source_target_pairs={{0,1},{1,0},{2,3},{3,2},{4,5},{5,4},{6,7},{7,6},{8,9},{9,8},{10,11... | collective-permute-start | bytes 1179656 | tf_op jit(solution)/shard_map/ppermute | solution.py:806
  131.6 13.3 %collective-permute-start.32 = (f32[2,2,96,256]{3,2,1,0:T(8,128)S(1)}, f32[2,2,96,256]{3,2,1,0:T(8,128)S(1)}, u32[]{:S(2)}, u32[]{:S(2)}) collective-permute-start(f32[2,2,96,256]{3,2,1,0:T(8,128)S(1)} %add_bitcast_fusion.4), channel_id=1, source_target_pairs={{0,6},{1,7},{2,4},{3,5},{4,2},{5,3},{6,0},{7,1},{8,14},{9,15},{10,... | collective-permute-start | bytes 1179656 | tf_op jit(solution)/shard_map/ppermute | solution.py:806
  142.4 10.8 %collective-permute-start.29 = (f32[2,96,512]{2,1,0:T(8,128)S(1)}, f32[2,96,512]{2,1,0:T(8,128)S(1)}, u32[]{:S(2)}, u32[]{:S(2)}) collective-permute-start(f32[2,96,512]{2,1,0:T(8,128)S(1)} %pad_maximum_fusion.2), channel_id=1, source_target_pairs={{0,2},{1,3},{2,0},{3,1},{4,6},{5,7},{6,4},{7,5},{8,10},{9,11},{10,... | collective-permute-start | bytes 1179656 | tf_op jit(solution)/shard_map/ppermute | solution.py:806
  144.9 6.2 %collective-permute-start.33 = (f32[2,96,256]{2,1,0:T(8,128)S(1)}, f32[2,96,256]{2,1,0:T(8,128)S(1)}, u32[]{:S(2)}, u32[]{:S(2)}) collective-permute-start(f32[2,96,256]{2,1,0:T(8,128)S(1)} %bitcast_add_fusion), channel_id=1, source_target_pairs={{0,1},{1,0},{2,3},{3,2},{4,5},{5,4},{6,7},{7,6},{8,9},{9,8},{10,11... | collective-permute-start | bytes 589832 | tf_op jit(solution)/shard_map/ppermute | solution.py:806
  153.4 7.5 %collective-permute-start.30 = (f32[96,512]{1,0:T(8,128)S(1)}, f32[96,512]{1,0:T(8,128)S(1)}, u32[]{:S(2)}, u32[]{:S(2)}) collective-permute-start(f32[96,512]{1,0:T(8,128)S(1)} %pad_maximum_fusion.37), channel_id=1, source_target_pairs={{0,6},{1,7},{2,4},{3,5},{4,2},{5,3},{6,0},{7,1},{8,14},{9,15},{10,... | collective-permute-start | bytes 589832 | tf_op jit(solution)/shard_map/ppermute | solution.py:806
  194.3 10.0 %collective-permute-start.3 = (f32[37,768]{1,0:T(8,128)S(1)}, f32[37,768]{1,0:T(8,128)S(1)}, u32[]{:S(2)}, u32[]{:S(2)}) collective-permute-start(f32[37,768]{1,0:T(8,128)S(1)} %concatenate.33), channel_id=1, source_target_pairs={{0,8},{1,9},{2,10},{3,11},{4,12},{5,13},{6,14},{7,15},{8,0},{9,1},... | collective-permute-start | bytes 341000 | tf_op jit(solution)/shard_map/ppermute | solution.py:806
  195.1 65.2 %collective-permute-start.21 = (f32[2,2,2,24,1024]{4,3,2,1,0:T(8,128)}, f32[2,2,2,24,1024]{4,3,2,1,0:T(8,128)}, u32[]{:S(2)}, u32[]{:S(2)}) collective-permute-start(f32[2,2,2,24,1024]{4,3,2,1,0:T(8,128)} %get-tuple-element.110), channel_id=1, source_target_pairs={{0,2},{1,3},{2,0},{3,1},{4,6},{5,7},{6,4},{7,5},{8,10},{9,11},{10,... | collective-permute-start | bytes 2359304 | tf_op jit(solution)/shard_map/ppermute | solution.py:806
  200.4 63.4 %collective-permute-start.15 = (f32[2,4,24,1408]{3,2,1,0:T(8,128)}, f32[2,4,24,1408]{3,2,1,0:T(8,128)}, u32[]{:S(2)}, u32[]{:S(2)}) collective-permute-start(f32[2,4,24,1408]{3,2,1,0:T(8,128)} %get-tuple-element.106), channel_id=1, source_target_pairs={{0,1},{1,0},{2,3},{3,2},{4,5},{5,4},{6,7},{7,6},{8,9},{9,8},{10,11... | collective-permute-start | bytes 3244040 | tf_op jit(solution)/shard_map/ppermute | solution.py:806
  203.0 63.0 %collective-permute-start.17 = (f32[4,2,24,1408]{3,2,0,1:T(8,128)}, f32[4,2,24,1408]{3,2,0,1:T(8,128)S(1)}, u32[]{:S(2)}, u32[]{:S(2)}) collective-permute-start(f32[4,2,24,1408]{3,2,0,1:T(8,128)} %copy.65), channel_id=1, source_target_pairs={{0,16},{1,17},{2,18},{3,19},{4,20},{5,21},{6,22},{7,23},{8,24},{9,... | collective-permute-start | bytes 3244040 | tf_op jit(solution)/shard_map/ppermute | solution.py:806
  204.3 25.0 %collective-permute-start.4 = (f32[37,768]{1,0:T(8,128)S(1)}, f32[37,768]{1,0:T(8,128)S(1)}, u32[]{:S(2)}, u32[]{:S(2)}) collective-permute-start(f32[37,768]{1,0:T(8,128)S(1)} %add.625), channel_id=1, source_target_pairs={{0,1},{1,0},{2,3},{3,2},{4,5},{5,4},{6,7},{7,6},{8,9},{9,8},{10,11... | collective-permute-start | bytes 341000 | tf_op jit(solution)/shard_map/ppermute | solution.py:806
  229.2 10.3 %collective-permute-start.5 = (f32[37,768]{1,0:T(8,128)S(1)}, f32[37,768]{1,0:T(8,128)S(1)}, u32[]{:S(2)}, u32[]{:S(2)}) collective-permute-start(f32[37,768]{1,0:T(8,128)S(1)} %add.626), channel_id=1, source_target_pairs={{0,16},{1,17},{2,18},{3,19},{4,20},{5,21},{6,22},{7,23},{8,24},{9,... | collective-permute-start | bytes 341000 | tf_op jit(solution)/shard_map/ppermute | solution.py:806
  244.5 6.7 %collective-permute-start.7 = (f32[37,768]{1,0:T(8,128)S(1)}, f32[37,768]{1,0:T(8,128)S(1)}, u32[]{:S(2)}, u32[]{:S(2)}) collective-permute-start(f32[37,768]{1,0:T(8,128)S(1)} %add.628), channel_id=1, source_target_pairs={{0,6},{1,7},{2,4},{3,5},{4,2},{5,3},{6,0},{7,1},{8,14},{9,15},{10,... | collective-permute-start | bytes 341000 | tf_op jit(solution)/shard_map/ppermute | solution.py:806
  247.6 44.1 %collective-permute-start.8 = (f32[3,384,768]{2,1,0:T(8,128)}, f32[3,384,768]{2,1,0:T(8,128)}, u32[]{:S(2)}, u32[]{:S(2)}) collective-permute-start(f32[3,384,768]{2,1,0:T(8,128)} %get-tuple-element.100), channel_id=1, source_target_pairs={{0,8},{1,9},{2,10},{3,11},{4,12},{5,13},{6,14},{7,15},{8,0},{9,1},... | collective-permute-start | bytes 10616840 | tf_op jit(solution)/shard_map/ppermute | solution.py:806
  261.4 9.9 %collective-permute-start.22 = (f32[2,2,24,1024]{3,2,1,0:T(8,128)S(1)}, f32[2,2,24,1024]{3,2,1,0:T(8,128)S(1)}, u32[]{:S(2)}, u32[]{:S(2)}) collective-permute-start(f32[2,2,24,1024]{3,2,1,0:T(8,128)S(1)} %add_bitcast_fusion.7), channel_id=1, source_target_pairs={{0,6},{1,7},{2,4},{3,5},{4,2},{5,3},{6,0},{7,1},{8,14},{9,15},{10,... | collective-permute-start | bytes 1179656 | tf_op jit(solution)/shard_map/ppermute | solution.py:806
  264.9 22.4 %collective-permute-start.16 = (f32[4,24,1408]{2,1,0:T(8,128)S(1)}, f32[4,24,1408]{2,1,0:T(8,128)S(1)}, u32[]{:S(2)}, u32[]{:S(2)}) collective-permute-start(f32[4,24,1408]{2,1,0:T(8,128)S(1)} %add_bitcast_fusion.1), channel_id=1, source_target_pairs={{0,16},{1,17},{2,18},{3,19},{4,20},{5,21},{6,22},{7,23},{8,24},{9,... | collective-permute-start | bytes 1622024 | tf_op jit(solution)/shard_map/ppermute | solution.py:806
  266.1 21.3 %collective-permute-start.18 = (f32[4,24,1408]{2,1,0:T(8,128)S(1)}, f32[4,24,1408]{2,1,0:T(8,128)S(1)}, u32[]{:S(2)}, u32[]{:S(2)}) collective-permute-start(f32[4,24,1408]{2,1,0:T(8,128)S(1)} %get-tuple-element.168), channel_id=1, source_target_pairs={{0,1},{1,0},{2,3},{3,2},{4,5},{5,4},{6,7},{7,6},{8,9},{9,8},{10,11... | collective-permute-start | bytes 1622024 | tf_op jit(solution)/shard_map/ppermute | solution.py:806
  272.3 8.5 %collective-permute-start.23 = (f32[2,24,1024]{2,1,0:T(8,128)S(1)}, f32[2,24,1024]{2,1,0:T(8,128)S(1)}, u32[]{:S(2)}, u32[]{:S(2)}) collective-permute-start(f32[2,24,1024]{2,1,0:T(8,128)S(1)} %bitcast_add_fusion.1), channel_id=1, source_target_pairs={{0,1},{1,0},{2,3},{3,2},{4,5},{5,4},{6,7},{7,6},{8,9},{9,8},{10,11... | collective-permute-start | bytes 589832 | tf_op jit(solution)/shard_map/ppermute | solution.py:806
  288.6 12.6 %collective-permute-start.19 = (f32[2,24,2816]{2,1,0:T(8,128)S(1)}, f32[2,24,2816]{2,1,0:T(8,128)S(1)}, u32[]{:S(2)}, u32[]{:S(2)}) collective-permute-start(f32[2,24,2816]{2,1,0:T(8,128)S(1)} %pad_maximum_fusion), channel_id=1, source_target_pairs={{0,2},{1,3},{2,0},{3,1},{4,6},{5,7},{6,4},{7,5},{8,10},{9,11},{10,... | collective-permute-start | bytes 1622024 | tf_op jit(solution)/shard_map/ppermute | solution.py:806
  299.6 18.9 %collective-permute-start.9 = (f32[2,4,24,1152]{3,2,1,0:T(8,128)}, f32[2,4,24,1152]{3,2,1,0:T(8,128)S(1)}, u32[]{:S(2)}, u32[]{:S(2)}) collective-permute-start(f32[2,4,24,1152]{3,2,1,0:T(8,128)} %get-tuple-element.102), channel_id=1, source_target_pairs={{0,1},{1,0},{2,3},{3,2},{4,5},{5,4},{6,7},{7,6},{8,9},{9,8},{10,11... | collective-permute-start | bytes 2654216 | tf_op jit(solution)/shard_map/ppermute | solution.py:806
  301.2 20.7 %collective-permute-start.11 = (f32[4,2,24,1152]{3,2,1,0:T(8,128)}, f32[4,2,24,1152]{3,2,1,0:T(8,128)S(1)}, u32[]{:S(2)}, u32[]{:S(2)}) collective-permute-start(f32[4,2,24,1152]{3,2,1,0:T(8,128)} %get-tuple-element.104), channel_id=1, source_target_pairs={{0,16},{1,17},{2,18},{3,19},{4,20},{5,21},{6,22},{7,23},{8,24},{9,... | collective-permute-start | bytes 2654216 | tf_op jit(solution)/shard_map/ppermute | solution.py:806
  302.4 28.6 %collective-permute-start.20 = (f32[24,2816]{1,0:T(8,128)S(1)}, f32[24,2816]{1,0:T(8,128)S(1)}, u32[]{:S(2)}, u32[]{:S(2)}) collective-permute-start(f32[24,2816]{1,0:T(8,128)S(1)} %pad_maximum_fusion.15), channel_id=1, source_target_pairs={{0,6},{1,7},{2,4},{3,5},{4,2},{5,3},{6,0},{7,1},{8,14},{9,15},{10,... | collective-permute-start | bytes 811016 | tf_op jit(solution)/shard_map/ppermute | solution.py:806
  318.5 8.4 %collective-permute-start.10 = (f32[4,24,1152]{2,1,0:T(8,128)S(1)}, f32[4,24,1152]{2,1,0:T(8,128)S(1)}, u32[]{:S(2)}, u32[]{:S(2)}) collective-permute-start(f32[4,24,1152]{2,1,0:T(8,128)S(1)} %add_bitcast_fusion.3), channel_id=1, source_target_pairs={{0,16},{1,17},{2,18},{3,19},{4,20},{5,21},{6,22},{7,23},{8,24},{9,... | collective-permute-start | bytes 1327112 | tf_op jit(solution)/shard_map/ppermute | solution.py:806
  321.9 8.4 %collective-permute-start.12 = (f32[4,24,1152]{2,1,0:T(8,128)S(1)}, f32[4,24,1152]{2,1,0:T(8,128)S(1)}, u32[]{:S(2)}, u32[]{:S(2)}) collective-permute-start(f32[4,24,1152]{2,1,0:T(8,128)S(1)} %add_bitcast_fusion.2), channel_id=1, source_target_pairs={{0,1},{1,0},{2,3},{3,2},{4,5},{5,4},{6,7},{7,6},{8,9},{9,8},{10,11... | collective-permute-start | bytes 1327112 | tf_op jit(solution)/shard_map/ppermute | solution.py:806
  330.6 10.7 %collective-permute-start.13 = (f32[2,24,2304]{2,1,0:T(8,128)S(1)}, f32[2,24,2304]{2,1,0:T(8,128)S(1)}, u32[]{:S(2)}, u32[]{:S(2)}) collective-permute-start(f32[2,24,2304]{2,1,0:T(8,128)S(1)} %pad_maximum_fusion.1), channel_id=1, source_target_pairs={{0,2},{1,3},{2,0},{3,1},{4,6},{5,7},{6,4},{7,5},{8,10},{9,11},{10,... | collective-permute-start | bytes 1327112 | tf_op jit(solution)/shard_map/ppermute | solution.py:806
  341.4 7.8 %collective-permute-start.14 = (f32[24,2304]{1,0:T(8,128)S(1)}, f32[24,2304]{1,0:T(8,128)S(1)}, u32[]{:S(2)}, u32[]{:S(2)}) collective-permute-start(f32[24,2304]{1,0:T(8,128)S(1)} %pad_maximum_fusion.26), channel_id=1, source_target_pairs={{0,6},{1,7},{2,4},{3,5},{4,2},{5,3},{6,0},{7,1},{8,14},{9,15},{10,... | collective-permute-start | bytes 663560 | tf_op jit(solution)/shard_map/ppermute | solution.py:806
  (33 other events, 219.5 us)
